TPU v7x, 128 devices: a whole 4x4x4 slice. The times are simulated.
128 devices in a mesh: pair: 8 (over z, core), virt: 16 (over y, x).
Axes of the slice: x: 4, y: 4, z: 4, core: 2. Of those that a mesh axis runs over, the one named last changes fastest.
Arguments:
- amplitudes: bfloat16 [8, 8, 2048, 2048], P('pair', None, 'virt'), may hold values from -6 to 6
- factor: bfloat16 [8192, 1024], P('virt'), may hold values from -0.125 to 0.125
- home: int32 [128], replicated, may hold values from 0 to 127, as said below
- domains: int32 [8, 32], P('pair'), may hold values from 0 to 127, as said below
- coupling: bfloat16 [1024, 1024], P('virt'), may hold values from -6 to 6
- hole_weight: bfloat16 [8, 3, 1024], P('pair', None, 'virt'), may hold values from -3 to 3
- virt_energy: float32 [8192], replicated, may hold values from 0.1 to 1
- occ_i: float32 [8], replicated, may hold values from -0.6 to -0.1
- occ_j: float32 [8], P('pair'), may hold values from -0.6 to -0.1
Outputs:
- residual: float32 [8, 8, 2048, 2048], P('pair', None, 'virt')
Inputs may be any that keep to these rules, and one draw needn't show every extreme that they name: `home`: a permutation of the virtual tiles; device k of virt stores the factor rows of slots k * 8 to (k + 1) * 8 - 1. `domains`: each row lists 32 distinct virtual tiles; at most 4 of a row's tiles are stored on any one device of virt, and in every row some device stores exactly 4 of them.
All inputs are finite; a program needn't handle non-finite values.
Results may differ from a plain program's by a relative error of at most 0.0033.
Values may be sent and summed in bfloat16 or wider, within the bound.
A program may use at most 128 MiB of HBM per device.

v0:
```python
import jax
import jax.numpy as jnp
from jax import lax
from jax.sharding import PartitionSpec as P

TILE = 64


def with_halo(array, sides, width):
    for axis, dim in sides:
        peers, length = (lax.axis_size(axis), array.shape[dim])
        up = [(i, (i + 1) % peers) for i in range(peers - 1)]
        down = [(j, i) for i, j in up]
        last = lax.slice_in_dim(array, length - width, length, axis=dim)
        first = lax.slice_in_dim(array, 0, width, axis=dim)
        before = lax.ppermute(last, axis, up)
        after = lax.ppermute(first, axis, down)
        array = jnp.concatenate([before, array, after], axis=dim)
    return array


def on_device(amplitudes, factor, home, domains, coupling, hole_weight, virt_energy, occ_i, occ_j):
    factor_cols = factor.shape[1]
    tile_total = home.shape[0]
    domain_entry_row = domains[0]
    slot_of = jnp.sum(
        jnp.where(
            home[None, :] == domain_entry_row[:, None],
            jnp.arange(tile_total, dtype=jnp.int32)[None, :],
            0,
        ),
        axis=1,
    )
    everything = lax.all_gather(factor, "virt", axis=0, tiled=True)
    domain_coefficient = everything.reshape(tile_total, TILE, factor_cols)[slot_of].reshape(
        -1, factor_cols
    )
    cluster_amplitude = amplitudes[0]
    half = jnp.einsum(
        "hjm,mf->hfj", cluster_amplitude, domain_coefficient, preferred_element_type=jnp.float32
    ).astype(jnp.bfloat16)
    projected = jnp.einsum(
        "iqd,dp->iqp",
        lax.all_to_all(half, "virt", split_axis=1, concat_axis=2, tiled=True),
        domain_coefficient,
        preferred_element_type=jnp.float32,
    ).astype(jnp.bfloat16)
    neighbours = with_halo(projected[None], (("pair", 0),), 1)
    weights = hole_weight[0].astype(jnp.float32)
    hole = (
        weights[0][None, :, None] * neighbours[0].astype(jnp.float32)
        + weights[1][None, :, None] * neighbours[1].astype(jnp.float32)
        + weights[2][None, :, None] * neighbours[2].astype(jnp.float32)
    )
    dressed = (coupling.astype(jnp.float32)[None] * projected.astype(jnp.float32) + hole).astype(
        jnp.bfloat16
    )
    back = jnp.einsum(
        "iqp,ap->iqa", dressed, domain_coefficient, preferred_element_type=jnp.float32
    ).astype(jnp.bfloat16)
    ladder = jnp.einsum(
        "iqa,bq->iab",
        lax.all_to_all(back, "virt", split_axis=2, concat_axis=1, tiled=True),
        domain_coefficient,
        preferred_element_type=jnp.float32,
    )
    rows_here = cluster_amplitude.shape[1]
    domain_width = cluster_amplitude.shape[2]
    spots = jnp.arange(domain_width, dtype=jnp.int32)
    orbitals = domain_entry_row[spots // TILE] * TILE + spots % TILE
    col_energy = virt_energy[orbitals]
    row_energy = lax.dynamic_slice_in_dim(col_energy, lax.axis_index("virt") * rows_here, rows_here)
    shift = row_energy[None, :, None] + col_energy[None, None, :] - occ_i[:, None, None] - occ_j[0]
    return (ladder + shift * cluster_amplitude.astype(jnp.float32))[None]


def solution(mesh):
    placed = (
        P("pair", None, "virt", None),
        P("virt", None),
        P(),
        P("pair", None),
        P("virt", None),
        P("pair", None, "virt"),
        P(),
        P(),
        P("pair"),
    )
    return jax.shard_map(
        on_device,
        mesh=mesh,
        in_specs=placed,
        out_specs=P("pair", None, "virt", None),
        check_vma=False,
    )
```

profile of v0, /device:TPU:1, one launch (start us, length us, event | category | flops | bytes accessed | tf_op | source)
XLA Modules:
  0.0 284.3 jit_solution(8291726338405408386)
XLA Ops:
  7.3 0.8 select_reduce_fusion
  8.1 115.8 %all-gather.2.cloned.1.call-done = bf16[8192,1024]{1,0:T(8,128)(2,1)} async-done(((bf16[512,1024]{1,0:T(8,128)(2,1)}), bf16[8192,1024]{1,0:T(8,128)(2,1)}) %all-gather.2.cloned.1.call-update) | async-done | bytes 16777232 | tf_op jit(solution)/shard_map/all_gather | solution.py:34
  123.9 8.5 %gather_fusion = bf16[32,64,1024]{2,1,0:T(8,128)(2,1)} fusion(bf16[128,64,1024]{2,1,0:T(8,128)(2,1)} %bitcast.104, s32[1024]{0:T(1024)S(1)} %pad_clamp_fusion), kind=kCustom, calls=%fused_computation | custom fusion | bytes 8388736 | tf_op jit(solution)/shard_map/gather | solution.py:35
  132.4 7.6 %convert_bitcast_fusion = bf16[8,1024,128]{2,1,0:T(8,128)(2,1)S(1)} fusion(bf16[2048,1024,1]{1,0,2:T(8,128)(2,1)} %bitcast.99, bf16[1,8,128,2048]{3,2,1,0:T(8,128)(2,1)} %param.9), kind=kOutput, calls=%fused_computation.15 | convolution fusion | flops 4296015872 | bytes 10485760 | tf_op jit(solution)/shard_map/hjm,mf->hfj/dot_general | solution.py:39
  140.0 1.4 copy.30
  141.4 32.2 %all_to_all.36 = bf16[8,1024,128]{2,0,1:T(8,128)(2,1)S(1)} all-to-all(bf16[8,1024,128]{2,0,1:T(8,128)(2,1)S(1)} %copy.30), channel_id=1, replica_groups=mesh['pair'=8,'virt'=16] {'virt'}, dimensions={1} | all-to-all | bytes 4194304 | tf_op jit(solution)/shard_map/all_to_all | solution.py:44
  173.6 1.4 copy.42
  174.9 2.3 all_to_all.29
  177.2 5.2 %convolution_convert_fusion.1 = bf16[8,64,1024]{2,1,0:T(8,128)(2,1)S(1)} fusion(bf16[8,64,2048]{2,1,0:T(8,128)(2,1)} %all_to_all.29, bf16[2048,1024,1]{1,0,2:T(8,128)(2,1)} %bitcast.100), kind=kOutput, calls=%fused_computation.16 | convolution fusion | flops 2148007936 | bytes 7340032 | tf_op jit(solution)/shard_map/iqd,dp->iqp/dot_general | solution.py:42
  182.4 3.9 %collective-permute-start.1 = (bf16[1,8,64,1024]{3,2,1,0:T(8,128)(2,1)S(1)}, bf16[1,8,64,1024]{3,2,1,0:T(8,128)(2,1)S(1)}, u32[]{:S(2)}, u32[]{:S(2)}) collective-permute-start(bf16[1,8,64,1024]{3,2,1,0:T(8,128)(2,1)S(1)} %bitcast.109), channel_id=1, source_target_pairs={{16,0},{32,16},{48,32},{64,48},{80,64},{96,80},{112,96},{17,1},{33... | collective-permute-start | bytes 3145736 | tf_op jit(solution)/shard_map/ppermute | solution.py:17
  186.3 3.1 %collective-permute-start = (bf16[1,8,64,1024]{3,2,1,0:T(8,128)(2,1)S(1)}, bf16[1,8,64,1024]{3,2,1,0:T(8,128)(2,1)}, u32[]{:S(2)}, u32[]{:S(2)}) collective-permute-start(bf16[1,8,64,1024]{3,2,1,0:T(8,128)(2,1)S(1)} %bitcast.110), channel_id=1, source_target_pairs={{0,16},{16,32},{32,48},{48,64},{64,80},{80,96},{96,112},{1,17},{17... | collective-permute-start | bytes 3145736 | tf_op jit(solution)/shard_map/ppermute | solution.py:16
  190.2 9.8 %collective-permute-done.1 = bf16[1,8,64,1024]{3,2,1,0:T(8,128)(2,1)S(1)} collective-permute-done((bf16[1,8,64,1024]{3,2,1,0:T(8,128)(2,1)S(1)}, bf16[1,8,64,1024]{3,2,1,0:T(8,128)(2,1)S(1)}, u32[]{:S(2)}, u32[]{:S(2)}) %collective-permute-start.1) | collective-permute-done | bytes 1048608 | tf_op jit(solution)/shard_map/ppermute | solution.py:17
  199.9 1.2 collective-permute-done
  201.1 5.5 %convolution_convert_fusion = bf16[8,64,2048]{2,1,0:T(8,128)(2,1)S(1)} fusion(bf16[2048,1024,1]{1,0,2:T(8,128)(2,1)} %bitcast.101, bf16[8,64,1024]{2,1,0:T(8,128)(2,1)S(1)} %convolution_convert_fusion.1, bf16[1,8,64,1024]{3,2,1,0:T(8,128)(2,1)} %copy-done.4, bf16[1,8,64,1024]{3,2,1,0:T(8,128)(2,1)} %collective-permute-done, f32[64]{0:T(128)S(1)} %get-tuple-element.6, ...), kind=kOutput, calls=%fused_computation.5 | convolution fusion | flops 2154299392 | bytes 9700096 | tf_op jit(solution)/shard_map/iqp,ap->iqa/dot_general | solution.py:58
  206.6 4.2 %copy.32 = bf16[8,64,2048]{1,0,2:T(8,128)(2,1)} copy(bf16[8,64,2048]{2,1,0:T(8,128)(2,1)S(1)} %convolution_convert_fusion) | data formatting | bytes 4194304 | tf_op jit(solution)/shard_map/convert_element_type | solution.py:60
  210.9 7.5 %reshape.378 = bf16[16,2,32768]{2,1,0:T(2,128)(2,1)} reshape(bf16[2048,8,64]{2,1,0:T(8,128)(2,1)} %bitcast.95) | data formatting | bytes 4194304
  218.4 3.7 %all-to-all-start.1 = ((bf16[16,2,32768]{2,1,0:T(2,128)(2,1)}), bf16[16,2,32768]{2,1,0:T(2,128)(2,1)S(1)}, u32[]{:S(2)}, u32[]{:S(2)}) async-start(bf16[16,2,32768]{2,1,0:T(2,128)(2,1)} %reshape.378), calls=%async_computation.1 | async-start | bytes 4194304 | tf_op jit(solution)/shard_map/all_to_all | solution.py:63
  224.1 0.7 fusion.17
  224.8 4.5 %compare_select_fusion.2 = s32[2048,1]{0,1:T(1,128)S(1)} fusion(s32[]{:T(128)} %bitcast.46, s32[]{:T(128)} %bitcast.47, s32[]{:T(128)} %bitcast.48, s32[]{:T(128)} %bitcast.49, s32[]{:T(128)} %bitcast.50, s32[]{:T(128)} %bitcast.52, s32[]{:T(128)} %bitcast.51), kind=kLoop, calls=%fused_computation.51 | loop fusion | flops 47104 | bytes 8220 | tf_op jit(solution)/shard_map/gather | solution.py:70
  229.3 15.5 %select_multiply_fusion = s32[2048]{0:T(1024)S(1)} fusion(pred[2048]{0:T(1024)(128)(4,1)S(1)} %compare_reduce_fusion, pred[2048]{0:T(1024)(128)(4,1)S(1)} %compare_reduce_fusion.1, pred[2048]{0:T(1024)(128)(4,1)S(1)} %compare_reduce_fusion.2, pred[2048]{0:T(1024)(128)(4,1)S(1)} %compare_reduce_fusion.3, pred[2048]{0:T(1024)(128)(4,1)S(1)} %compare_reduce_fusion.4, ...), kind=kLoop, calls=%fused_computation.64 | loop fusion | flops 53248 | bytes 67684 | tf_op jit(solution)/shard_map/mul | solution.py:70
  244.9 11.8 %gather_fusion.1 = f32[2048]{0:T(1024)S(1)} fusion(f32[8192]{0:T(1024)S(1)} %copy-done, s32[2048]{0:T(1024)S(1)} %broadcast_clamp_fusion), kind=kCustom, calls=%fused_computation.1 | custom fusion | bytes 24576 | tf_op jit(solution)/shard_map/gather | solution.py:71
  256.9 5.0 %reshape.379 = bf16[2048,8,64]{2,1,0:T(8,128)(2,1)} reshape(bf16[16,2,32768]{2,1,0:T(2,128)(2,1)S(1)} %all-to-all-done.1) | data formatting | bytes 4194304
  261.9 4.7 %copy.34 = bf16[8,16,64,128]{3,2,1,0:T(8,128)(2,1)S(1)} copy(bf16[8,16,64,128]{2,0,3,1:T(8,128)(2,1)} %bitcast.96) | data formatting | bytes 4194304 | tf_op jit(solution)/shard_map/all_to_all | solution.py:63
  266.5 10.9 %add_bitcast_fusion = f32[1,8,128,2048]{3,2,1,0:T(8,128)} fusion(bf16[1,8,128,2048]{3,2,1,0:T(8,128)(2,1)} %param.9, f32[]{:T(128)} %bitcast.94, f32[8]{0:T(128)S(1)} %copy-done.5, f32[128,2048]{1,0:T(8,128)S(1)} %broadcast_add_fusion, bf16[8,1024,128]{2,1,0:T(8,128)(2,1)S(1)} %bitcast.103, bf16[2048,1024,1]{1,0,2:T(8,128)(2,1)} %bitcast.102), kind=kOutput, calls=%fused_computation.2 | convolution fusion | flops 4305453056 | bytes 19922980 | tf_op jit(solution)/shard_map/iqa,bq->iab/dot_general | solution.py:61
  (50 shorter events, 3.1 us)
Async XLA Ops:
  6.5 238.3 %copy-start = (f32[8192]{0:T(1024)S(1)}, f32[8192]{0:T(1024)}, u32[]{:S(2)}) copy-start(f32[8192]{0:T(1024)} %param.15) | copy-start | bytes 98308
  6.5 117.4 %all-gather.2.cloned.1.call-start = ((), (), s32[]{:S(2)}) async-start(), calls=%async_computation.2 | async-start | bytes 17825792 | tf_op jit(solution)/shard_map/all_gather | solution.py:34
  177.2 12.8 %copy-start.3 = (bf16[1,3,64]{2,1,0:T(4,128)(2,1)S(1)}, bf16[1,3,64]{2,1,0:T(4,128)(2,1)}, u32[]{:S(2)}) copy-start(bf16[1,3,64]{2,1,0:T(4,128)(2,1)} %param.14) | copy-start | bytes 1156
  177.2 12.9 %copy-start.2 = (bf16[64,1024]{1,0:T(8,128)(2,1)S(1)}, bf16[64,1024]{1,0:T(8,128)(2,1)}, u32[]{:S(2)}) copy-start(bf16[64,1024]{1,0:T(8,128)(2,1)} %param.13) | copy-start | bytes 393220
  182.4 17.5 %collective-permute-start.1 = (bf16[1,8,64,1024]{3,2,1,0:T(8,128)(2,1)S(1)}, bf16[1,8,64,1024]{3,2,1,0:T(8,128)(2,1)S(1)}, u32[]{:S(2)}, u32[]{:S(2)}) collective-permute-start(bf16[1,8,64,1024]{3,2,1,0:T(8,128)(2,1)S(1)} %bitcast.109), channel_id=1, source_target_pairs={{16,0},{32,16},{48,32},{64,48},{80,64},{96,80},{112,96},{17,1},{33... | collective-permute-start | bytes 3145736 | tf_op jit(solution)/shard_map/ppermute | solution.py:17
  186.3 14.8 %collective-permute-start = (bf16[1,8,64,1024]{3,2,1,0:T(8,128)(2,1)S(1)}, bf16[1,8,64,1024]{3,2,1,0:T(8,128)(2,1)}, u32[]{:S(2)}, u32[]{:S(2)}) collective-permute-start(bf16[1,8,64,1024]{3,2,1,0:T(8,128)(2,1)S(1)} %bitcast.110), channel_id=1, source_target_pairs={{0,16},{16,32},{32,48},{48,64},{64,80},{80,96},{96,112},{1,17},{17... | collective-permute-start | bytes 3145736 | tf_op jit(solution)/shard_map/ppermute | solution.py:16
  199.9 1.2 copy-start.4
  210.9 12.6 %copy-start.1 = (s32[1,32]{1,0:T(1,128)S(1)}, s32[1,32]{1,0:T(1,128)}, u32[]{:S(2)}) copy-start(s32[1,32]{1,0:T(1,128)} %param.12) | copy-start | bytes 388
  218.4 38.5 %all-to-all-start.1 = ((bf16[16,2,32768]{2,1,0:T(2,128)(2,1)}), bf16[16,2,32768]{2,1,0:T(2,128)(2,1)S(1)}, u32[]{:S(2)}, u32[]{:S(2)}) async-start(bf16[16,2,32768]{2,1,0:T(2,128)(2,1)} %reshape.378), calls=%async_computation.1 | async-start | bytes 4194304 | tf_op jit(solution)/shard_map/all_to_all | solution.py:63
  261.9 4.7 %copy-start.5 = (f32[8]{0:T(128)S(1)}, f32[8]{0:T(128)}, u32[]{:S(2)}) copy-start(f32[8]{0:T(128)} %param.16) | copy-start | bytes 100
Sparse Core Ops, SparseCore 0:
  9.5 114.3 all-gather.1
where the time goes:
time: 285 us; the launch traced here: 284 us
  waiting for transfers between devices  127 us (45%)
  local copies, waits for them, and re-layouts  48.2 us (17%)
  blocking collectives  32.2 us (11%)
  matrix products  29.2 us (10%)
  other arithmetic  22.4 us (8%)
  between operations  14.2 us (5%)
  starting transfers between devices  10.7 us (4%)
    all_gather x1, waiting for transfers between devices, on_device(): everything = lax.all_gather(factor, 'virt', axis=0, tiled=True)  116 us
    all_to_all x1, blocking collectives, on_device(): lax.all_to_all(half, 'virt', split_axis=1, concat_axis=2, tiled=True)  32.2 us
    mul x1, other arithmetic, on_device(): orbitals = domain_entry_row[spots // TILE] * TILE + spots % TILE  15.5 us
    unnamed x14, local copies, waits for them, and re-layouts  12.5 us
    gather x1, local copies, waits for them, and re-layouts, on_device(): col_energy = virt_energy[orbitals]  11.8 us
    dot_general x1, matrix products, on_device(): jnp.einsum('iqa,bq->iab', lax.all_to_all(back, 'virt', split_axis=2, conc...  10.9 us
    ppermute x1, waiting for transfers between devices, with_halo(): after = lax.ppermute(first, axis, down)  9.77 us
    gather x1, local copies, waits for them, and re-layouts, on_device(): everything.reshape(tile_total, TILE, factor_cols)[slot_of]  8.51 us
  transfers between devices with their start and end apart: 4, of which 3 were waited for; matrix products, arithmetic and copies ran while one was open for 13% of the time, Pallas kernels for 0%

commit v1 on v0

v1 whole, which is shorter than its diff:
```python
import jax
import jax.numpy as jnp
from jax import lax
from jax.experimental import pallas as pl
from jax.experimental.pallas import tpu as pltpu
from jax.sharding import PartitionSpec as P

TILE = 64
CAP = 4
SIDE = 4
PLANE = SIDE * SIDE
CHUNK = 2
MESH = pl.DeviceIdType.MESH
NT = (((1,), (1,)), ((), ()))
NN = (((1,), (0,)), ((), ()))
TN = (((0,), (0,)), ((), ()))


def dot(a, b, dims):
    return lax.dot_general(a, b, dims, preferred_element_type=jnp.float32)


def exchange_kernel(
    local_ref,
    place_ref,
    factor_ref,
    amp_hbm,
    coupling_ref,
    weight_ref,
    dt_out,
    back_out,
    amp,
    pack,
    got,
    dt,
    hbuf,
    recvh,
    proj,
    below,
    above,
    dressed,
    bbuf,
    io_sem,
    pack_sem,
    got_sem,
    ag_send,
    ag_recv,
    h_send,
    h_recv,
    p_send,
    below_sem,
    above_sem,
    b_send,
    b_recv,
):
    pairs = lax.axis_size("pair")
    pair = lax.axis_index("pair")
    me = lax.axis_index("virt")
    y, x = lax.div(me, SIDE), lax.rem(me, SIDE)
    after = lax.rem(pair + 1, pairs)
    before = lax.rem(pair + pairs - 1, pairs)
    blk = dt.shape[0] // PLANE
    rows = amp.shape[0] // hbuf.shape[0]
    chunks = hbuf.shape[0] // CHUNK

    barrier = pltpu.get_barrier_semaphore()

    @pl.loop(1, PLANE)
    def _(s):
        pl.semaphore_signal(
            barrier, inc=1, device_id=(pair, lax.rem(me + s, PLANE)), device_id_type=MESH
        )

    pl.semaphore_signal(barrier, inc=1, device_id=(after, me), device_id_type=MESH)
    pl.semaphore_signal(barrier, inc=1, device_id=(before, me), device_id_type=MESH)

    load = pltpu.make_async_copy(amp_hbm, amp, io_sem.at[0])
    load.start()

    for c in range(CAP // 2):
        two = jnp.concatenate(
            [factor_ref[local_ref[2 * c]], factor_ref[local_ref[2 * c + 1]]], axis=0
        )
        pack[c] = two.T

    pl.semaphore_wait(barrier, PLANE + 1)

    def pack_part(d):
        return pack.at[:, pl.ds(pl.multiple_of(d * blk, blk), blk), :]

    here = got.at[pl.ds(me * (CAP // 2), CAP // 2)]

    @pl.loop(1, PLANE)
    def _(s):
        d = lax.rem(me + s, PLANE)
        pltpu.make_async_remote_copy(
            pack_part(d), here, pack_sem, got_sem, device_id=(pair, d), device_id_type=MESH
        ).start()

    pltpu.make_async_copy(pack_part(me), here, got_sem).start()
    pltpu.make_async_copy(got, got, got_sem).wait()

    def pick(t):
        wide = got[place_ref[0, t]]
        return jnp.where(place_ref[1, t] == 1, wide[:, TILE:], wide[:, :TILE])

    own = pl.ds(pl.multiple_of(me * blk, blk), blk)
    for u in range(dt.shape[1] // (2 * TILE)):
        dt[own, u * 2 * TILE : (u + 1) * 2 * TILE] = jnp.concatenate(
            [pick(2 * u), pick(2 * u + 1)], axis=1
        )

    def at(axis, along, across):
        dx, dy = (along, across) if axis == 0 else (across, along)
        return lax.rem(y + dy + SIDE, SIDE) * SIDE + lax.rem(x + dx + SIDE, SIDE)

    hb, qb = blk // 2, blk // 4
    names = {}

    def message(kind, h, s, sign):
        k = names.setdefault((kind, h, s, sign), len(names))
        if kind == "a1":
            block, to = at(h, 0, 0), at(h, sign, 0)
        elif kind == "a2":
            block, to = at(h, -sign, 0), at(h, sign, 0)
        elif kind == "b1":
            block, to = at(h, s, 0), at(h, 0, sign)
        else:
            block, to = at(h, s, -sign), at(h, 0, sign)
        if kind in ("a1", "b1"):
            off, n = h * hb, hb
        else:
            off, n = h * hb + (0 if sign > 0 else qb), qb
        part = dt.at[pl.ds(pl.multiple_of(block * blk + off, qb), n), :]
        return pltpu.make_async_remote_copy(
            part, part, ag_send.at[k], ag_recv.at[k], device_id=(pair, to), device_id_type=MESH
        )

    def each(kind, offsets, do):
        for s in offsets:
            for h in (0, 1):
                for sign in (1, -1):
                    do(message(kind, h, s, sign))

    def go(m):
        m.start()

    def landed(m):
        m.wait_recv()

    each("a1", (0,), go)
    each("b1", (0,), go)
    for h in (0, 1):
        for sign in (1, -1):
            message("a1", h, 0, sign).wait_recv()
            message("a2", h, 0, sign).start()
    each("b1", (1, -1), go)
    each("b1", (0,), landed)
    each("b2", (0,), go)
    each("a2", (0,), landed)
    each("b1", (2,), go)
    each("b1", (1, -1), landed)
    each("b2", (1, -1), go)
    each("b1", (2,), landed)
    each("b2", (2,), go)
    each("b2", (0, 1, -1, 2), landed)

    store = pltpu.make_async_copy(dt, dt_out, io_sem.at[1])
    store.start()
    load.wait()

    def send(src, dst, send_sem, recv_sem, d):
        @pl.when(d != me)
        def _():
            pltpu.make_async_remote_copy(
                src, dst, send_sem, recv_sem, device_id=(pair, d), device_id_type=MESH
            ).start()

        @pl.when(d == me)
        def _():
            pltpu.make_async_copy(src, dst, recv_sem).start()

    @pl.loop(0, chunks)
    def _(c):
        now = pl.ds(c * CHUNK, CHUNK)

        @pl.loop(0, SIDE)
        def _(k):
            r = lax.rem(y + k, SIDE)
            band = pl.ds(pl.multiple_of(r * SIDE * blk, SIDE * blk), SIDE * blk)
            lines = pl.ds(pl.multiple_of(c * CHUNK * rows, CHUNK * rows), CHUNK * rows)
            part = dot(dt[band, :], amp[lines, :], NT).astype(jnp.bfloat16)
            for i in range(CHUNK):
                hbuf[c * CHUNK + i, band, :] = part[:, i * rows : (i + 1) * rows]
            for w in range(SIDE):
                d = r * SIDE + lax.rem(x + w, SIDE)
                send(
                    hbuf.at[now, pl.ds(pl.multiple_of(d * blk, blk), blk), :],
                    recvh.at[now, :, pl.ds(pl.multiple_of(me * rows, rows), rows)],
                    h_send,
                    h_recv.at[c],
                    d,
                )

    def project(c):
        now = pl.ds(c * CHUNK, CHUNK)
        pltpu.make_async_copy(recvh.at[now], recvh.at[now], h_recv.at[c]).wait()
        left = recvh[now].reshape(CHUNK * blk, recvh.shape[2])
        step = 256
        for n in range(dt.shape[0] // step):
            cols = slice(n * step, (n + 1) * step)
            part = dot(left, dt[cols, :], NT).astype(jnp.bfloat16)
            proj[now, :, cols] = part.reshape(CHUNK, blk, step)
        pltpu.make_async_remote_copy(
            proj.at[now], below.at[now], p_send.at[0], below_sem.at[c],
            device_id=(after, me), device_id_type=MESH,
        ).start()
        pltpu.make_async_remote_copy(
            proj.at[now], above.at[now], p_send.at[1], above_sem.at[c],
            device_id=(before, me), device_id_type=MESH,
        ).start()

    def finish(c):
        now = pl.ds(c * CHUNK, CHUNK)
        pltpu.make_async_copy(below.at[now], below.at[now], below_sem.at[c]).wait()
        pltpu.make_async_copy(above.at[now], above.at[now], above_sem.at[c]).wait()
        f32 = jnp.float32
        for i in range(CHUNK):
            mine = proj[c * CHUNK + i].astype(f32)
            hole = (
                weight_ref[0] * below[c * CHUNK + i].astype(f32)
                + weight_ref[1] * mine
                + weight_ref[2] * above[c * CHUNK + i].astype(f32)
            )
            dressed[i * blk : (i + 1) * blk, :] = (
                coupling_ref[...].astype(f32) * mine + hole
            ).astype(jnp.bfloat16)

        @pl.loop(0, PLANE // 2)
        def _(k):
            two = lax.rem(lax.div(me, 2) + k, PLANE // 2)
            cols = pl.ds(pl.multiple_of(two * 2 * rows, 2 * rows), 2 * rows)
            part = dot(dressed[...], dt[:, cols], NN).astype(jnp.bfloat16)
            bbuf[now, :, cols] = part.reshape(CHUNK, blk, 2 * rows)
            for w in range(2):
                d = two * 2 + w
                send(
                    bbuf.at[now, :, pl.ds(pl.multiple_of(d * rows, rows), rows)],
                    back_out.at[now, own, :],
                    b_send,
                    b_recv,
                    d,
                )

    @pl.loop(0, chunks + 1)
    def _(c):
        @pl.when(c < chunks)
        def _():
            project(c)

        @pl.when(c > 0)
        def _():
            finish(c - 1)

    pltpu.make_async_copy(back_out, back_out, b_recv).wait()
    store.wait()

    def sent(ref, sem):
        pltpu.make_async_copy(ref, ref, sem).wait()

    sent(pack.at[:, pl.ds(blk, (PLANE - 1) * blk), :], pack_sem)
    sent(hbuf.at[:, pl.ds(blk, (PLANE - 1) * blk), :], h_send)
    sent(proj, p_send.at[0])
    sent(proj, p_send.at[1])
    sent(bbuf.at[:, :, pl.ds(rows, (PLANE - 1) * rows)], b_send)
    for kind, offsets in (("a1", (0,)), ("a2", (0,)), ("b1", (0, 1, -1, 2)), ("b2", (0, 1, -1, 2))):
        each(kind, offsets, lambda m: m.wait_send())


def ladder_kernel(occ_i_ref, occ_j_ref, back_ref, dt_ref, amp_ref, col_ref, row_ref, out_ref):
    step = pl.program_id(0)
    n = back_ref.shape[0]
    rows = back_ref.shape[2]
    left = jnp.concatenate([back_ref[i].T for i in range(n)], axis=0)
    shift = row_ref[...] + col_ref[...]
    wide = 512
    for b in range(dt_ref.shape[1] // wide):
        cols = slice(b * wide, (b + 1) * wide)
        part = dot(left, dt_ref[:, cols], NN)
        for i in range(n):
            out_ref[i, :, cols] = part[i * rows : (i + 1) * rows] + (
                shift[:, cols] - occ_i_ref[step * n + i] - occ_j_ref[0]
            ) * amp_ref[i, :, cols].astype(jnp.float32)


def on_device(amplitudes, factor, home, domains, coupling, hole_weight, virt_energy, occ_i, occ_j):
    pairs = lax.axis_size("pair")
    pair = lax.axis_index("pair")
    me = lax.axis_index("virt")
    amps = amplitudes[0]
    ni, rows, width = amps.shape
    stored, rank = factor.shape
    tiles_here = stored // TILE
    blk = rank // PLANE
    domain = domains[0]
    tiles = home.shape[0]

    slot = jnp.sum(
        jnp.where(
            home[None, :] == domain[:, None], jnp.arange(tiles, dtype=jnp.int32)[None, :], 0
        ),
        axis=1,
    )
    holder = slot // tiles_here
    order = jnp.arange(domain.shape[0], dtype=jnp.int32)
    nth = jnp.sum(
        ((holder[None, :] == holder[:, None]) & (order[None, :] < order[:, None])).astype(jnp.int32),
        axis=1,
    )
    local = jnp.sum(
        jnp.where(
            (holder == me)[None, :] & (nth[None, :] == jnp.arange(CAP, dtype=jnp.int32)[:, None]),
            (slot % tiles_here)[None, :],
            0,
        ),
        axis=1,
    )
    place = jnp.stack([holder * (CAP // 2) + nth // 2, nth % 2])

    weight = hole_weight[0].astype(jnp.float32)
    weight = jnp.stack(
        [
            jnp.where(pair > 0, weight[0], 0.0),
            weight[1],
            jnp.where(pair < pairs - 1, weight[2], 0.0),
        ]
    )[:, :, None]

    by_tile = virt_energy.reshape(tiles, TILE)
    col = jnp.sum(
        jnp.where(
            domain[:, None, None] == jnp.arange(tiles, dtype=jnp.int32)[None, :, None],
            by_tile[None],
            0.0,
        ),
        axis=1,
    ).reshape(width)
    row = lax.dynamic_slice_in_dim(col, me * rows, rows)

    bf16 = jnp.bfloat16
    smem = pl.BlockSpec(memory_space=pltpu.SMEM)
    vmem = pl.BlockSpec(memory_space=pltpu.VMEM)
    anywhere = pl.BlockSpec(memory_space=pl.ANY)
    dma = pltpu.SemaphoreType.DMA
    chunks = ni // CHUNK
    dt, back = pl.pallas_call(
        exchange_kernel,
        out_shape=(
            jax.ShapeDtypeStruct((rank, width), bf16),
            jax.ShapeDtypeStruct((ni, rank, rows), bf16),
        ),
        in_specs=[smem, smem, vmem, anywhere, vmem, vmem],
        out_specs=(anywhere, anywhere),
        scratch_shapes=[
            pltpu.VMEM((ni * rows, width), bf16),
            pltpu.VMEM((CAP // 2, rank, 2 * TILE), bf16),
            pltpu.VMEM((PLANE * CAP // 2, blk, 2 * TILE), bf16),
            pltpu.VMEM((rank, width), bf16),
            pltpu.VMEM((ni, rank, rows), bf16),
            pltpu.VMEM((ni, blk, width), bf16),
            pltpu.VMEM((ni, blk, rank), bf16),
            pltpu.VMEM((ni, blk, rank), bf16),
            pltpu.VMEM((ni, blk, rank), bf16),
            pltpu.VMEM((CHUNK * blk, rank), bf16),
            pltpu.VMEM((ni, blk, width), bf16),
            dma((2,)),
            dma,
            dma,
            dma((40,)),
            dma((40,)),
            dma,
            dma((chunks,)),
            dma((2,)),
            dma((chunks,)),
            dma((chunks,)),
            dma,
            dma,
        ],
        compiler_params=pltpu.CompilerParams(
            collective_id=0, has_side_effects=True, vmem_limit_bytes=48 * 2**20
        ),
    )(
        local,
        place,
        factor.reshape(tiles_here, TILE, rank),
        amps.reshape(ni * rows, width),
        coupling,
        weight,
    )

    n = 2
    residual = pl.pallas_call(
        ladder_kernel,
        grid=(ni // n,),
        out_shape=jax.ShapeDtypeStruct((ni, rows, width), jnp.float32),
        in_specs=[
            smem,
            smem,
            pl.BlockSpec((n, rank, rows), lambda i: (i, 0, 0)),
            pl.BlockSpec((rank, width), lambda i: (0, 0)),
            pl.BlockSpec((n, rows, width), lambda i: (i, 0, 0)),
            pl.BlockSpec((1, width), lambda i: (0, 0)),
            pl.BlockSpec((rows, 1), lambda i: (0, 0)),
        ],
        out_specs=pl.BlockSpec((n, rows, width), lambda i: (i, 0, 0)),
        compiler_params=pltpu.CompilerParams(vmem_limit_bytes=32 * 2**20),
    )(occ_i, occ_j, back, dt, amps, col[None, :], row[:, None])
    return residual[None]


def solution(mesh):
    placed = (
        P("pair", None, "virt", None),
        P("virt", None),
        P(),
        P("pair", None),
        P("virt", None),
        P("pair", None, "virt"),
        P(),
        P(),
        P("pair"),
    )
    return jax.shard_map(
        on_device,
        mesh=mesh,
        in_specs=placed,
        out_specs=P("pair", None, "virt", None),
        check_vma=False,
    )
```

time: 285 us -> 105 us (0.37)
  waiting for transfers between devices: 127 us -> 0 us
  Pallas kernels: 0 us -> 94.9 us
  local copies, waits for them, and re-layouts: 48.2 us -> 5.66 us
  blocking collectives: 32.2 us -> 0 us
  matrix products: 29.2 us -> 0 us
  other arithmetic: 22.4 us -> 3 us
  between operations: 14.2 us -> 0.74 us
  starting transfers between devices: 10.7 us -> 0 us
    all_gather x1 -> x0, waiting for transfers between devices: 116 us -> none  [on_device(): everything = lax.all_gather(factor, 'virt', axis=0, tiled=True)]
    pallas_call x0 -> x2, Pallas kernels: none -> 94.9 us  [the longest x1 87.4 us: on_device(): pl.pallas_call(exchange_kernel, out_shape=(jax.ShapeDtypeStruct((rank, wi...]
    all_to_all x1 -> x0, blocking collectives: 32.2 us -> none  [on_device(): lax.all_to_all(half, 'virt', split_axis=1, concat_axis=2, tiled=True)]
    dot_general x4 -> x0, matrix products: 29.2 us -> none  [the longest x1 10.9 us: on_device(): jnp.einsum('iqa,bq->iab', lax.all_to_all(back, 'virt', split_axis=2, conc...]
    gather x4 -> x0, local copies, waits for them, and re-layouts: 21.7 us -> none  [the longest x1 11.8 us: on_device(): col_energy = virt_energy[orbitals]]
    mul x1 -> x0, other arithmetic: 15.5 us -> none  [on_device(): orbitals = domain_entry_row[spots // TILE] * TILE + spots % TILE]
    ppermute x2 -> x0, waiting for transfers between devices: 10.9 us -> none  [the longest x1 9.77 us: with_halo(): after = lax.ppermute(first, axis, down)]
    all_to_all x3 -> x0, local copies, waits for them, and re-layouts: 8.3 us -> none  [the longest x1 4.66 us: on_device(): lax.all_to_all(back, 'virt', split_axis=2, concat_axis=1, tiled=True)]
  transfers between devices with their start and end apart: 4 -> 0, of which waited for: 3 -> 0; matrix products, arithmetic and copies ran while one was open for 13% -> 0% of each run, Pallas kernels for 0% -> 0%
where the time goes in v1:
time: 105 us; the launch traced here: 104 us
  Pallas kernels  94.9 us (90%)
  local copies, waits for them, and re-layouts  5.66 us (5%)
  other arithmetic  3 us (3%)
    pallas_call x1, Pallas kernels, on_device(): pl.pallas_call(exchange_kernel, out_shape=(jax.ShapeDtypeStruct((rank, wi...  87.4 us
    pallas_call x1, Pallas kernels, on_device(): pl.pallas_call(ladder_kernel, grid=(ni // n,), out_shape=jax.ShapeDtypeSt...  7.45 us
    unnamed x10, local copies, waits for them, and re-layouts  4.32 us

profile of v1, /device:TPU:1, one launch (start us, length us, event | category | flops | bytes accessed | tf_op | source)
XLA Modules:
  0.0 104.3 jit_solution(11855168425665693385)
XLA Ops:
  0.0 0.0 copy-start.4
  0.7 0.8 select_reduce_fusion.1
  1.6 0.2 convert_reduce_fusion
  1.7 0.1 select_reduce_fusion.2.local_ref
  1.9 0.7 convert_element_type.8
  2.6 0.7 iota_compare_fusion
  3.3 0.8 broadcast_in_dim.78
  4.2 0.1 copy.14
  4.2 0.4 select_reduce_fusion
  4.6 0.1 reshape.211
  4.7 0.1 broadcast_in_dim_reshape.4.col_ref
  4.7 0.1 dynamic-slice_bitcast_fusion
  4.8 0.1 copy.15.row_ref
  4.9 0.1 copy.13.weight_ref
  5.0 0.0 copy-start.2
  5.1 1.2 %copy-done.2 = bf16[512,1024]{1,0:T(8,128)(2,1)S(1)} copy-done((bf16[512,1024]{1,0:T(8,128)(2,1)S(1)}, bf16[512,1024]{1,0:T(8,128)(2,1)}, u32[]{:S(2)}) %copy-start.2) | copy-done | bytes 1048600
  6.3 0.0 copy-start.3
  6.3 0.9 copy-done.3
  7.2 87.4 %shard_map.91 = (bf16[1024,2048]{1,0:T(8,128)(2,1)}, bf16[8,1024,128]{2,1,0:T(8,128)(2,1)S(1)}) custom-call(s32[4]{0:T(128)S(1)} %select_reduce_fusion.2.local_ref, s32[2,32]{1,0:T(2,128)S(1)} %pad_add_fusion.place_ref, bf16[8,64,1024]{2,1,0:T(8,128)(2,1)S(1)} %bitcast.44, bf16[1024,2048]{1,0:T(8,128)(2,1)} %bitcast.42, bf16[64,1024]{1,0:T(8,128)(2,1)S(1)} %copy-done.3, ...), custom_call_target="tpu_custom_call" | custom-call | tf_op jit(solution)/shard_map/pallas_call | solution.py:356
  94.6 0.0 copy-done.4
  94.6 0.0 copy-done
  94.6 0.0 copy-start.1
  94.7 2.2 %copy-done.1 = bf16[1024,2048]{1,0:T(8,128)(2,1)S(1)} copy-done((bf16[1024,2048]{1,0:T(8,128)(2,1)S(1)}, bf16[1024,2048]{1,0:T(8,128)(2,1)}, u32[]{:S(2)}) %copy-start.1) | copy-done | bytes 4194328
  96.8 7.4 %shard_map.92 = f32[8,128,2048]{2,1,0:T(8,128)} custom-call(f32[8]{0:T(128)S(1)} %copy-done.4, f32[1]{0:T(128)S(6)} %copy.16.occ_j_ref, bf16[8,1024,128]{2,1,0:T(8,128)(2,1)S(1)} %get-tuple-element.7.back_ref, bf16[1024,2048]{1,0:T(8,128)(2,1)S(1)} %copy-done.1, bf16[8,128,2048]{2,1,0:T(8,128)(2,1)S(1)} %bitcast.43, ...), custom_call_target="tpu_custom_call" | custom-call | tf_op jit(solution)/shard_map/pallas_call | solution.py:402
  (7 shorter events, 0.1 us)
Async XLA Ops:
  0.0 94.6 %copy-start.4 = (f32[8]{0:T(128)S(1)}, f32[8]{0:T(128)}, u32[]{:S(2)}) copy-start(f32[8]{0:T(128)} %occ_i_ref.1) | copy-start | bytes 100
  5.0 1.2 %copy-start.2 = (bf16[512,1024]{1,0:T(8,128)(2,1)S(1)}, bf16[512,1024]{1,0:T(8,128)(2,1)}, u32[]{:S(2)}) copy-start(bf16[512,1024]{1,0:T(8,128)(2,1)} %param.10) | copy-start | bytes 3145732
  6.3 0.9 copy-start.3
  7.2 87.4 %copy-start = (bf16[1,8,128,2048]{3,2,1,0:T(8,128)(2,1)S(1)}, bf16[1,8,128,2048]{3,2,1,0:T(8,128)(2,1)}, u32[]{:S(2)}) copy-start(bf16[1,8,128,2048]{3,2,1,0:T(8,128)(2,1)} %param.9) | copy-start | bytes 12582916
  94.6 2.2 %copy-start.1 = (bf16[1024,2048]{1,0:T(8,128)(2,1)S(1)}, bf16[1024,2048]{1,0:T(8,128)(2,1)}, u32[]{:S(2)}) copy-start(bf16[1024,2048]{1,0:T(8,128)(2,1)} %get-tuple-element.8.dt_ref) | copy-start | bytes 12582916

commit v2 on v1

v2 whole, which is shorter than its diff:
```python
import jax
import jax.numpy as jnp
from jax import lax
from jax.experimental import pallas as pl
from jax.experimental.pallas import tpu as pltpu
from jax.sharding import PartitionSpec as P

TILE = 64
CAP = 4
SIDE = 4
PLANE = SIDE * SIDE
CHUNK = 2
MESH = pl.DeviceIdType.MESH
NT = (((1,), (1,)), ((), ()))
NN = (((1,), (0,)), ((), ()))


def dot(a, b, dims):
    return lax.dot_general(a, b, dims, preferred_element_type=jnp.float32)


def residual_kernel(
    factor_hbm,
    home_hbm,
    domain_hbm,
    amp_hbm,
    coupling_hbm,
    weight_hbm,
    energy_hbm,
    occ_i_hbm,
    occ_j,
    out_ref,
    factor,
    home,
    domain,
    amp,
    coupling,
    weight,
    energy,
    occ_i,
    table,
    where,
    columns,
    col,
    row,
    pack,
    got,
    dt,
    hbuf,
    recvh,
    proj,
    below,
    above,
    dressed,
    bbuf,
    recvb,
    io_sem,
    pack_sem,
    got_sem,
    ag_send,
    ag_recv,
    h_send,
    h_recv,
    p_send,
    below_sem,
    above_sem,
    b_send,
    b_recv,
):
    f32, bf16, i32 = jnp.float32, jnp.bfloat16, jnp.int32
    pairs = lax.axis_size("pair")
    pair = lax.axis_index("pair")
    me = lax.axis_index("virt")
    y, x = lax.div(me, SIDE), lax.rem(me, SIDE)
    after = lax.rem(pair + 1, pairs)
    before = lax.rem(pair + pairs - 1, pairs)
    rank, width = dt.shape
    blk = rank // PLANE
    rows = width // PLANE
    chunks = hbuf.shape[0] // CHUNK
    tiles_here = factor.shape[0]
    in_domain = width // TILE

    barrier = pltpu.get_barrier_semaphore()

    @pl.loop(1, PLANE)
    def _(s):
        pl.semaphore_signal(
            barrier, inc=1, device_id=(pair, lax.rem(me + s, PLANE)), device_id_type=MESH
        )

    pl.semaphore_signal(barrier, inc=1, device_id=(after, me), device_id_type=MESH)
    pl.semaphore_signal(barrier, inc=1, device_id=(before, me), device_id_type=MESH)

    def fetch(k, src, dst):
        copy = pltpu.make_async_copy(src, dst, io_sem.at[k])
        copy.start()
        return copy

    get_home = fetch(0, home_hbm, home)
    get_domain = fetch(1, domain_hbm, domain)
    get_factor = fetch(2, factor_hbm, factor)
    get_small = [
        fetch(3, coupling_hbm, coupling),
        fetch(4, weight_hbm, weight),
        fetch(5, energy_hbm, energy),
        fetch(6, occ_i_hbm, occ_i),
    ]
    get_amp = fetch(7, amp_hbm, amp)

    get_home.wait()
    get_domain.wait()
    tiles = home.shape[1]
    home_row = jnp.broadcast_to(home[...], (in_domain, tiles))
    domain_row = jnp.broadcast_to(domain[...], (tiles, in_domain))
    slots = lax.broadcasted_iota(i32, (in_domain, tiles), 1)
    slot_col = jnp.max(jnp.where(home_row == domain_row.T, slots, 0), axis=1, keepdims=True)
    slots = lax.broadcasted_iota(i32, (tiles, in_domain), 0)
    slot_row = jnp.max(jnp.where(home_row.T == domain_row, slots, 0), axis=0, keepdims=True)
    holder_col, holder_row = lax.div(slot_col, tiles_here), lax.div(slot_row, tiles_here)
    same = holder_col == holder_row
    up = lax.broadcasted_iota(i32, (in_domain, in_domain), 0)
    across = lax.broadcasted_iota(i32, (in_domain, in_domain), 1)
    nth_row = jnp.sum(jnp.where(same & (up < across), 1, 0), axis=0, keepdims=True)
    nth_col = jnp.sum(jnp.where(same & (across < up), 1, 0), axis=1, keepdims=True)
    nth_row, nth_col = jnp.minimum(nth_row, CAP - 1), jnp.minimum(nth_col, CAP - 1)
    number = lax.broadcasted_iota(i32, (in_domain, 128), 1)
    mine = jnp.max(
        jnp.where(
            (holder_col == me) & (nth_col == number), lax.rem(slot_col, tiles_here), 0
        ),
        axis=0,
        keepdims=True,
    )
    table[0:1, 0:in_domain] = holder_row * (CAP // 2) + lax.div(nth_row, 2)
    table[1:2, 0:in_domain] = lax.rem(nth_row, 2)
    table[2:3, 0:in_domain] = lax.div(domain[...], 2)
    table[3:4, 0:in_domain] = lax.rem(domain[...], 2)
    table[4:5, :] = mine
    table[5:8, :] = jnp.zeros((3, 128), i32)
    scalars = fetch(0, table, where)
    scalars.wait()

    get_factor.wait()
    for c in range(CAP // 2):
        two = jnp.concatenate([factor[where[4, 2 * c]], factor[where[4, 2 * c + 1]]], axis=0)
        pack[c] = two.T

    pl.semaphore_wait(barrier, PLANE + 1)

    def pack_part(d):
        return pack.at[:, pl.ds(pl.multiple_of(d * blk, blk), blk), :]

    here = got.at[pl.ds(me * (CAP // 2), CAP // 2)]

    @pl.loop(1, PLANE)
    def _(s):
        d = lax.rem(me + s, PLANE)
        pltpu.make_async_remote_copy(
            pack_part(d), here, pack_sem, got_sem, device_id=(pair, d), device_id_type=MESH
        ).start()

    pltpu.make_async_copy(pack_part(me), here, got_sem).start()

    for copy in get_small:
        copy.wait()

    def halves(wide, second):
        return jnp.where(second == 1, wide[:, TILE:], wide[:, :TILE])

    def energy_of(t):
        return halves(energy[pl.ds(where[2, t], 1), :], where[3, t])

    for u in range(in_domain // 2):
        col[:, u * 2 * TILE : (u + 1) * 2 * TILE] = jnp.concatenate(
            [energy_of(2 * u), energy_of(2 * u + 1)], axis=1
        )
    here_energy = col[:, pl.ds(pl.multiple_of(me * rows, rows), rows)]
    row[...] = jnp.broadcast_to(here_energy, (rows, rows)).T - occ_j[0]
    has = (jnp.where(pair > 0, 1.0, 0.0), 1.0, jnp.where(pair < pairs - 1, 1.0, 0.0))
    for d in range(3):
        line = weight[d : d + 1, :].astype(f32) * has[d]
        columns[d] = jnp.broadcast_to(line, (128, blk)).T

    pltpu.make_async_copy(got, got, got_sem).wait()

    own = pl.ds(pl.multiple_of(me * blk, blk), blk)

    def tile_of(t):
        return halves(got[where[0, t]], where[1, t])

    for u in range(in_domain // 2):
        dt[own, u * 2 * TILE : (u + 1) * 2 * TILE] = jnp.concatenate(
            [tile_of(2 * u), tile_of(2 * u + 1)], axis=1
        )

    def device(dy, dx):
        return lax.rem(y + dy + SIDE, SIDE) * SIDE + lax.rem(x + dx + SIDE, SIDE)

    def at(axis, along, other):
        return device(other, along) if axis == 0 else device(along, other)

    hb, qb = blk // 2, blk // 4
    names = {}

    def message(kind, h, s, sign):
        k = names.setdefault((kind, h, s, sign), len(names))
        if kind == "a1":
            block, to = at(h, 0, 0), at(h, sign, 0)
        elif kind == "a2":
            block, to = at(h, -sign, 0), at(h, sign, 0)
        elif kind == "b1":
            block, to = at(h, s, 0), at(h, 0, sign)
        else:
            block, to = at(h, s, -sign), at(h, 0, sign)
        if kind in ("a1", "b1"):
            off, n = h * hb, hb
        else:
            off, n = h * hb + (0 if sign > 0 else qb), qb
        part = dt.at[pl.ds(pl.multiple_of(block * blk + off, qb), n), :]
        return pltpu.make_async_remote_copy(
            part, part, ag_send.at[k], ag_recv.at[k], device_id=(pair, to), device_id_type=MESH
        )

    def each(kind, offsets, do):
        for s in offsets:
            for h in (0, 1):
                for sign in (1, -1):
                    do(message(kind, h, s, sign))

    def go(m):
        m.start()

    def landed(m):
        m.wait_recv()

    def send(src, dst, send_sem, recv_sem, d):
        pltpu.make_async_remote_copy(
            src, dst, send_sem, recv_sem, device_id=(pair, d), device_id_type=MESH
        ).start()

    def band_of(d):
        return pl.ds(pl.multiple_of(d * blk, blk), blk)

    def half_parts(c, d):
        now = pl.ds(c * CHUNK, CHUNK)
        return (
            hbuf.at[now, band_of(d), :],
            recvh.at[now, :, pl.ds(pl.multiple_of(me * rows, rows), rows)],
        )

    def half(c, owners):
        left = jnp.concatenate([dt[band_of(d), :] for d in owners], axis=0)
        lines = pl.ds(pl.multiple_of(c * CHUNK * rows, CHUNK * rows), CHUNK * rows)
        part = dot(left, amp[lines, :], NT).astype(bf16)
        for k, d in enumerate(owners):
            for i in range(CHUNK):
                hbuf[c * CHUNK + i, band_of(d), :] = part[
                    k * blk : (k + 1) * blk, i * rows : (i + 1) * rows
                ]

    def half_send(c, owners):
        for d in owners:
            src, dst = half_parts(c, d)
            send(src, dst, h_send, h_recv.at[c], d)

    in_row = [device(0, k) for k in range(1, SIDE)]
    in_column = [device(k, 0) for k in range(1, SIDE)]

    each("a1", (0,), go)
    each("b1", (0,), go)
    for h in (0, 1):
        for sign in (1, -1):
            message("a1", h, 0, sign).wait_recv()
            message("a2", h, 0, sign).start()
    each("b1", (1, -1), go)
    each("b1", (0,), landed)
    each("b2", (0,), go)
    each("a2", (0,), landed)
    each("b1", (2,), go)
    each("b2", (0,), landed)
    get_amp.wait()

    @pl.loop(0, chunks)
    def _(c):
        half(c, [me, *in_row])
        half(c, in_column)

    each("b1", (1, -1), landed)
    each("b2", (1, -1), go)
    each("b1", (2,), landed)
    each("b2", (2,), go)

    @pl.loop(0, chunks)
    def _(c):
        src, dst = half_parts(c, me)
        pltpu.make_async_copy(src, dst, h_recv.at[c]).start()
        half_send(c, [d for two in zip(in_row, in_column) for d in two])

    each("b2", (1, -1, 2), landed)

    @pl.loop(0, chunks)
    def _(c):
        @pl.loop(1, SIDE)
        def _(k):
            owners = [device(k, w) for w in range(1, SIDE)]
            half(c, owners)
            half_send(c, owners)

    def project(c):
        now = pl.ds(c * CHUNK, CHUNK)
        pltpu.make_async_copy(recvh.at[now], recvh.at[now], h_recv.at[c]).wait()
        left = recvh[now].reshape(CHUNK * blk, width)
        step = 256
        for n in range(rank // step):
            cols = slice(n * step, (n + 1) * step)
            part = dot(left, dt[cols, :], NT).astype(bf16)
            proj[now, :, cols] = part.reshape(CHUNK, blk, step)
        pltpu.make_async_remote_copy(
            proj.at[now], below.at[now], p_send.at[0], below_sem.at[c],
            device_id=(after, me), device_id_type=MESH,
        ).start()
        pltpu.make_async_remote_copy(
            proj.at[now], above.at[now], p_send.at[1], above_sem.at[c],
            device_id=(before, me), device_id_type=MESH,
        ).start()

    def finish(c):
        now = pl.ds(c * CHUNK, CHUNK)
        pltpu.make_async_copy(below.at[now], below.at[now], below_sem.at[c]).wait()
        pltpu.make_async_copy(above.at[now], above.at[now], above_sem.at[c]).wait()
        for i in range(CHUNK):
            mid = proj[c * CHUNK + i].astype(f32)
            hole = (
                columns[0][:, :1] * below[c * CHUNK + i].astype(f32)
                + columns[1][:, :1] * mid
                + columns[2][:, :1] * above[c * CHUNK + i].astype(f32)
            )
            dressed[i * blk : (i + 1) * blk, :] = (
                coupling[...].astype(f32) * mid + hole
            ).astype(bf16)

        @pl.loop(0, PLANE // 2)
        def _(k):
            two = lax.rem(lax.div(me, 2) + k, PLANE // 2)
            cols = pl.ds(pl.multiple_of(two * 2 * rows, 2 * rows), 2 * rows)
            part = dot(dressed[...], dt[:, cols], NN).astype(bf16)
            bbuf[now, :, cols] = part.reshape(CHUNK, blk, 2 * rows)
            for w in range(2):
                d = two * 2 + w
                src = bbuf.at[now, :, pl.ds(pl.multiple_of(d * rows, rows), rows)]
                dst = recvb.at[now, own, :]

                @pl.when(d != me)
                def _():
                    send(src, dst, b_send, b_recv.at[c], d)

                @pl.when(d == me)
                def _():
                    pltpu.make_async_copy(src, dst, b_recv.at[c]).start()

    @pl.loop(0, chunks + 1)
    def _(c):
        @pl.when(c < chunks)
        def _():
            project(c)

        @pl.when(c > 0)
        def _():
            finish(c - 1)

    @pl.loop(0, chunks)
    def _(c):
        now = pl.ds(c * CHUNK, CHUNK)
        pltpu.make_async_copy(recvb.at[now], recvb.at[now], b_recv.at[c]).wait()
        left = jnp.concatenate([recvb[c * CHUNK + i].T for i in range(CHUNK)], axis=0)
        wide = 512
        for b in range(width // wide):
            cols = slice(b * wide, (b + 1) * wide)
            part = dot(left, dt[:, cols], NN)
            for i in range(CHUNK):
                lines = pl.ds(pl.multiple_of((c * CHUNK + i) * rows, rows), rows)
                shift = row[:, :1] + (col[:, cols] - occ_i[c * CHUNK + i])
                out_ref[c * CHUNK + i, :, cols] = part[
                    i * rows : (i + 1) * rows
                ] + shift * amp[lines, cols].astype(f32)

    def sent(ref, sem):
        pltpu.make_async_copy(ref, ref, sem).wait()

    sent(pack.at[:, pl.ds(blk, (PLANE - 1) * blk), :], pack_sem)
    sent(hbuf.at[:, pl.ds(blk, (PLANE - 1) * blk), :], h_send)
    sent(proj, p_send.at[0])
    sent(proj, p_send.at[1])
    sent(bbuf.at[:, :, pl.ds(rows, (PLANE - 1) * rows)], b_send)
    for kind, offsets in (("a1", (0,)), ("a2", (0,)), ("b1", (0, 1, -1, 2)), ("b2", (0, 1, -1, 2))):
        each(kind, offsets, lambda m: m.wait_send())


def on_device(amplitudes, factor, home, domains, coupling, hole_weight, virt_energy, occ_i, occ_j):
    ni, rows, width = amplitudes.shape[1:]
    stored, rank = factor.shape
    tiles_here = stored // TILE
    tiles = home.shape[0]
    blk = rank // PLANE
    lines = virt_energy.shape[0] // (2 * TILE)

    f32, bf16, i32 = jnp.float32, jnp.bfloat16, jnp.int32
    dma = pltpu.SemaphoreType.DMA
    chunks = ni // CHUNK
    residual = pl.pallas_call(
        residual_kernel,
        out_shape=pltpu.VMEM((ni, rows, width), f32),
        in_specs=[pl.BlockSpec(memory_space=pltpu.HBM)] * 8
        + [pl.BlockSpec(memory_space=pltpu.SMEM)],
        out_specs=pl.BlockSpec(memory_space=pltpu.VMEM),
        scratch_shapes=[
            pltpu.VMEM((tiles_here, TILE, rank), bf16),
            pltpu.VMEM((1, tiles), i32),
            pltpu.VMEM(domains.shape, i32),
            pltpu.VMEM((ni * rows, width), bf16),
            pltpu.VMEM((blk, rank), bf16),
            pltpu.VMEM((3, blk), bf16),
            pltpu.VMEM((lines, 2 * TILE), f32),
            pltpu.SMEM((ni,), f32),
            pltpu.VMEM((8, 128), i32),
            pltpu.SMEM((8, 128), i32),
            pltpu.VMEM((3, blk, 128), f32),
            pltpu.VMEM((1, width), f32),
            pltpu.VMEM((rows, rows), f32),
            pltpu.VMEM((CAP // 2, rank, 2 * TILE), bf16),
            pltpu.VMEM((PLANE * CAP // 2, blk, 2 * TILE), bf16),
            pltpu.VMEM((rank, width), bf16),
            pltpu.VMEM((ni, rank, rows), bf16),
            pltpu.VMEM((ni, blk, width), bf16),
            pltpu.VMEM((ni, blk, rank), bf16),
            pltpu.VMEM((ni, blk, rank), bf16),
            pltpu.VMEM((ni, blk, rank), bf16),
            pltpu.VMEM((CHUNK * blk, rank), bf16),
            pltpu.VMEM((ni, blk, width), bf16),
            pltpu.VMEM((ni, rank, rows), bf16),
            dma((8,)),
            dma,
            dma,
            dma((40,)),
            dma((40,)),
            dma,
            dma((chunks,)),
            dma((2,)),
            dma((chunks,)),
            dma((chunks,)),
            dma,
            dma((chunks,)),
        ],
        compiler_params=pltpu.CompilerParams(
            collective_id=0, has_side_effects=True, vmem_limit_bytes=48 * 2**20
        ),
    )(
        factor.reshape(tiles_here, TILE, rank),
        home[None, :],
        domains,
        amplitudes.reshape(ni * rows, width),
        coupling,
        hole_weight[0],
        virt_energy.reshape(lines, 2 * TILE),
        occ_i,
        occ_j,
    )
    return residual[None]


def solution(mesh):
    placed = (
        P("pair", None, "virt", None),
        P("virt", None),
        P(),
        P("pair", None),
        P("virt", None),
        P("pair", None, "virt"),
        P(),
        P(),
        P("pair"),
    )
    return jax.shard_map(
        on_device,
        mesh=mesh,
        in_specs=placed,
        out_specs=P("pair", None, "virt", None),
        check_vma=False,
    )
```

time: 105 us -> 95.1 us (0.906)
  Pallas kernels: 94.9 us -> 91 us
  other arithmetic: 3 us -> 0 us
  local copies, waits for them, and re-layouts: 5.66 us -> 3.4 us
    pallas_call x2 -> x1, Pallas kernels: 94.9 us -> 91 us  [on_device(): pl.pallas_call(residual_kernel, out_shape=pltpu.VMEM((ni, rows, width), f...]
    reduce_sum x4 -> x0, other arithmetic: 1.52 us -> none  [the longest x1 0.85 us: on_device(): jnp.sum(jnp.where(home[None, :] == domain[:, None], jnp.arange(tiles, dty...]
    broadcast_in_dim x5 -> x0, local copies, waits for them, and re-layouts: 1.2 us -> none  [the longest x2 0.89 us: on_device(): jnp.where(domain[:, None, None] == jnp.arange(tiles, dtype=jnp.int32)[Non...]
    unnamed x10 -> x1, local copies, waits for them, and re-layouts: 4.32 us -> 3.4 us
where the time goes in v2:
time: 95.1 us; the launch traced here: 95 us
  Pallas kernels  91 us (96%)
  local copies, waits for them, and re-layouts  3.4 us (4%)
    pallas_call x1, Pallas kernels, on_device(): pl.pallas_call(residual_kernel, out_shape=pltpu.VMEM((ni, rows, width), f...  91 us
    unnamed x1, local copies, waits for them, and re-layouts  3.4 us

profile of v2, /device:TPU:1, one launch (start us, length us, event | category | flops | bytes accessed | tf_op | source)
XLA Modules:
  0.0 95.0 jit_solution(4036869055455433321)
XLA Ops:
  0.7 91.0 %shard_map.91 = f32[8,128,2048]{2,1,0:T(8,128)S(1)} custom-call(bf16[8,64,1024]{2,1,0:T(8,128)(2,1)} %bitcast.8, s32[1,128]{1,0:T(1,128)} %bitcast.11, s32[1,32]{1,0:T(1,128)} %domain_hbm.1, bf16[1024,2048]{1,0:T(8,128)(2,1)} %bitcast.7, bf16[64,1024]{1,0:T(8,128)(2,1)} %coupling_hbm.1, bf16[3,64]{1,0:T(4,128)(2,1)} %bitcast.10, f32[64,128]{1,0:T(8,128)} %bitcast.9, ...), custom_call_target="tpu_custom_call" | custom-call | tf_op jit(solution)/shard_map/pallas_call | solution.py:411
  91.6 3.4 %copy.11 = f32[1,8,128,2048]{3,2,1,0:T(8,128)} copy(f32[1,8,128,2048]{3,2,1,0:T(8,128)S(1)} %bitcast.6) | data formatting | bytes 16777216

commit v3 on v2

--- a/solution.py
+++ b/solution.py
@@ -17,6 +17,43 @@
 
 def dot(a, b, dims):
     return lax.dot_general(a, b, dims, preferred_element_type=jnp.float32)
+
+
+def ladder_steps(width):
+    return [slice(b, b + 512) for b in range(0, width, 512)]
+
+
+def ladder_left(recvb, c):
+    return jnp.concatenate([recvb[c * CHUNK + i].T for i in range(CHUNK)], axis=0)
+
+
+def ladder_part(left, c, cols, dt, amp, col, row, occ_i, out, slot):
+    rows = left.shape[0] // CHUNK
+    part = dot(left, dt[:, cols], NN)
+    for i in range(CHUNK):
+        lines = pl.ds(pl.multiple_of((c * CHUNK + i) * rows, rows), rows)
+        shift = row[:, :1] + (col[:, cols] - occ_i[c * CHUNK + i])
+        out[slot * CHUNK + i, :, cols] = part[i * rows : (i + 1) * rows] + shift * amp[
+            lines, cols
+        ].astype(jnp.float32)
+
+
+def last_kernel(occ_i, ladder, amp, dt, recvb, col, row, out_hbm, last, sem, last_sem):
+    done = ladder.shape[0]
+    c = done // CHUNK
+    copies = [pltpu.make_async_copy(ladder.at[i], out_hbm.at[i], sem.at[i]) for i in range(done)]
+    for copy in copies:
+        copy.start()
+    left = ladder_left(recvb, c)
+    for k, cols in enumerate(ladder_steps(dt.shape[1])):
+        ladder_part(left, c, cols, dt, amp, col, row, occ_i, last, 0)
+        copy = pltpu.make_async_copy(
+            last.at[:, :, cols], out_hbm.at[pl.ds(done, CHUNK), :, cols], last_sem.at[k]
+        )
+        copy.start()
+        copies.append(copy)
+    for copy in copies:
+        copy.wait()
 
 
 def residual_kernel(
@@ -29,11 +66,15 @@
     energy_hbm,
     occ_i_hbm,
     occ_j,
-    out_ref,
+    ladder,
+    amp,
+    dt,
+    recvb,
+    col,
+    row,
     factor,
     home,
     domain,
-    amp,
     coupling,
     weight,
     energy,
@@ -41,11 +82,9 @@
     table,
     where,
     columns,
-    col,
-    row,
     pack,
-    got,
-    dt,
+    got_up,
+    got_low,
     hbuf,
     recvh,
     proj,
@@ -53,7 +92,6 @@
     above,
     dressed,
     bbuf,
-    recvb,
     io_sem,
     pack_sem,
     got_sem,
@@ -148,19 +186,24 @@
 
     pl.semaphore_wait(barrier, PLANE + 1)
 
-    def pack_part(d):
-        return pack.at[:, pl.ds(pl.multiple_of(d * blk, blk), blk), :]
-
-    here = got.at[pl.ds(me * (CAP // 2), CAP // 2)]
-
-    @pl.loop(1, PLANE)
-    def _(s):
-        d = lax.rem(me + s, PLANE)
-        pltpu.make_async_remote_copy(
-            pack_part(d), here, pack_sem, got_sem, device_id=(pair, d), device_id_type=MESH
-        ).start()
-
-    pltpu.make_async_copy(pack_part(me), here, got_sem).start()
+    hb, qb = blk // 2, blk // 4
+    got = (got_up, got_low)
+
+    def pack_part(d, h):
+        return pack.at[:, pl.ds(pl.multiple_of(d * blk + h * hb, hb), hb), :]
+
+    for h in range(2):
+        here = got[h].at[pl.ds(me * (CAP // 2), CAP // 2)]
+
+        @pl.loop(1, PLANE)
+        def _(s):
+            d = lax.rem(me + s, PLANE)
+            pltpu.make_async_remote_copy(
+                pack_part(d, h), here, pack_sem, got_sem.at[h],
+                device_id=(pair, d), device_id_type=MESH,
+            ).start()
+
+        pltpu.make_async_copy(pack_part(me, h), here, got_sem.at[h]).start()
 
     for copy in get_small:
         copy.wait()
@@ -182,17 +225,15 @@
         line = weight[d : d + 1, :].astype(f32) * has[d]
         columns[d] = jnp.broadcast_to(line, (128, blk)).T
 
-    pltpu.make_async_copy(got, got, got_sem).wait()
-
     own = pl.ds(pl.multiple_of(me * blk, blk), blk)
 
-    def tile_of(t):
-        return halves(got[where[0, t]], where[1, t])
-
-    for u in range(in_domain // 2):
-        dt[own, u * 2 * TILE : (u + 1) * 2 * TILE] = jnp.concatenate(
-            [tile_of(2 * u), tile_of(2 * u + 1)], axis=1
-        )
+    def arrange(h):
+        pltpu.make_async_copy(got[h], got[h], got_sem.at[h]).wait()
+        lines = pl.ds(pl.multiple_of(me * blk + h * hb, hb), hb)
+        for u in range(in_domain // 2):
+            dt[lines, u * 2 * TILE : (u + 1) * 2 * TILE] = jnp.concatenate(
+                [halves(got[h][where[0, t]], where[1, t]) for t in (2 * u, 2 * u + 1)], axis=1
+            )
 
     def device(dy, dx):
         return lax.rem(y + dy + SIDE, SIDE) * SIDE + lax.rem(x + dx + SIDE, SIDE)
@@ -200,7 +241,6 @@
     def at(axis, along, other):
         return device(other, along) if axis == 0 else device(along, other)
 
-    hb, qb = blk // 2, blk // 4
     names = {}
 
     def message(kind, h, s, sign):
@@ -235,40 +275,41 @@
         m.wait_recv()
 
     def send(src, dst, send_sem, recv_sem, d):
-        pltpu.make_async_remote_copy(
-            src, dst, send_sem, recv_sem, device_id=(pair, d), device_id_type=MESH
-        ).start()
+        @pl.when(d != me)
+        def _():
+            pltpu.make_async_remote_copy(
+                src, dst, send_sem, recv_sem, device_id=(pair, d), device_id_type=MESH
+            ).start()
+
+        @pl.when(d == me)
+        def _():
+            pltpu.make_async_copy(src, dst, recv_sem).start()
 
     def band_of(d):
         return pl.ds(pl.multiple_of(d * blk, blk), blk)
 
-    def half_parts(c, d):
+    def half(c, r):
         now = pl.ds(c * CHUNK, CHUNK)
-        return (
-            hbuf.at[now, band_of(d), :],
-            recvh.at[now, :, pl.ds(pl.multiple_of(me * rows, rows), rows)],
-        )
-
-    def half(c, owners):
-        left = jnp.concatenate([dt[band_of(d), :] for d in owners], axis=0)
+        band = pl.ds(pl.multiple_of(r * SIDE * blk, SIDE * blk), SIDE * blk)
         lines = pl.ds(pl.multiple_of(c * CHUNK * rows, CHUNK * rows), CHUNK * rows)
-        part = dot(left, amp[lines, :], NT).astype(bf16)
-        for k, d in enumerate(owners):
-            for i in range(CHUNK):
-                hbuf[c * CHUNK + i, band_of(d), :] = part[
-                    k * blk : (k + 1) * blk, i * rows : (i + 1) * rows
-                ]
-
-    def half_send(c, owners):
-        for d in owners:
-            src, dst = half_parts(c, d)
-            send(src, dst, h_send, h_recv.at[c], d)
-
-    in_row = [device(0, k) for k in range(1, SIDE)]
-    in_column = [device(k, 0) for k in range(1, SIDE)]
-
-    each("a1", (0,), go)
-    each("b1", (0,), go)
+        part = dot(dt[band, :], amp[lines, :], NT).astype(bf16)
+        for i in range(CHUNK):
+            hbuf[c * CHUNK + i, band, :] = part[:, i * rows : (i + 1) * rows]
+        for w in range(SIDE):
+            d = r * SIDE + lax.rem(x + w, SIDE)
+            send(
+                hbuf.at[now, band_of(d), :],
+                recvh.at[now, :, pl.ds(pl.multiple_of(me * rows, rows), rows)],
+                h_send,
+                h_recv.at[c],
+                d,
+            )
+
+    for h in (0, 1):
+        arrange(h)
+        for kind in ("a1", "b1"):
+            for sign in (1, -1):
+                message(kind, h, 0, sign).start()
     for h in (0, 1):
         for sign in (1, -1):
             message("a1", h, 0, sign).wait_recv()
@@ -279,33 +320,19 @@
     each("a2", (0,), landed)
     each("b1", (2,), go)
     each("b2", (0,), landed)
-    get_amp.wait()
-
-    @pl.loop(0, chunks)
-    def _(c):
-        half(c, [me, *in_row])
-        half(c, in_column)
-
     each("b1", (1, -1), landed)
     each("b2", (1, -1), go)
     each("b1", (2,), landed)
     each("b2", (2,), go)
 
+    each("b2", (1, -1, 2), landed)
+    get_amp.wait()
+
     @pl.loop(0, chunks)
     def _(c):
-        src, dst = half_parts(c, me)
-        pltpu.make_async_copy(src, dst, h_recv.at[c]).start()
-        half_send(c, [d for two in zip(in_row, in_column) for d in two])
-
-    each("b2", (1, -1, 2), landed)
-
-    @pl.loop(0, chunks)
-    def _(c):
-        @pl.loop(1, SIDE)
+        @pl.loop(0, SIDE)
         def _(k):
-            owners = [device(k, w) for w in range(1, SIDE)]
-            half(c, owners)
-            half_send(c, owners)
+            half(c, lax.rem(y + k, SIDE))
 
     def project(c):
         now = pl.ds(c * CHUNK, CHUNK)
@@ -340,24 +367,16 @@
                 coupling[...].astype(f32) * mid + hole
             ).astype(bf16)
 
-        @pl.loop(0, PLANE // 2)
+        @pl.loop(0, SIDE)
         def _(k):
-            two = lax.rem(lax.div(me, 2) + k, PLANE // 2)
-            cols = pl.ds(pl.multiple_of(two * 2 * rows, 2 * rows), 2 * rows)
+            r = lax.rem(y + k, SIDE)
+            cols = pl.ds(pl.multiple_of(r * SIDE * rows, SIDE * rows), SIDE * rows)
             part = dot(dressed[...], dt[:, cols], NN).astype(bf16)
-            bbuf[now, :, cols] = part.reshape(CHUNK, blk, 2 * rows)
-            for w in range(2):
-                d = two * 2 + w
+            bbuf[now, :, cols] = part.reshape(CHUNK, blk, SIDE * rows)
+            for w in range(SIDE):
+                d = r * SIDE + lax.rem(x + w, SIDE)
                 src = bbuf.at[now, :, pl.ds(pl.multiple_of(d * rows, rows), rows)]
-                dst = recvb.at[now, own, :]
-
-                @pl.when(d != me)
-                def _():
-                    send(src, dst, b_send, b_recv.at[c], d)
-
-                @pl.when(d == me)
-                def _():
-                    pltpu.make_async_copy(src, dst, b_recv.at[c]).start()
+                send(src, recvb.at[now, own, :], b_send, b_recv.at[c], d)
 
     @pl.loop(0, chunks + 1)
     def _(c):
@@ -373,17 +392,12 @@
     def _(c):
         now = pl.ds(c * CHUNK, CHUNK)
         pltpu.make_async_copy(recvb.at[now], recvb.at[now], b_recv.at[c]).wait()
-        left = jnp.concatenate([recvb[c * CHUNK + i].T for i in range(CHUNK)], axis=0)
-        wide = 512
-        for b in range(width // wide):
-            cols = slice(b * wide, (b + 1) * wide)
-            part = dot(left, dt[:, cols], NN)
-            for i in range(CHUNK):
-                lines = pl.ds(pl.multiple_of((c * CHUNK + i) * rows, rows), rows)
-                shift = row[:, :1] + (col[:, cols] - occ_i[c * CHUNK + i])
-                out_ref[c * CHUNK + i, :, cols] = part[
-                    i * rows : (i + 1) * rows
-                ] + shift * amp[lines, cols].astype(f32)
+
+        @pl.when(c < chunks - 1)
+        def _():
+            left = ladder_left(recvb, c)
+            for cols in ladder_steps(width):
+                ladder_part(left, c, cols, dt, amp, col, row, occ_i, ladder, c)
 
     def sent(ref, sem):
         pltpu.make_async_copy(ref, ref, sem).wait()
@@ -408,17 +422,26 @@
     f32, bf16, i32 = jnp.float32, jnp.bfloat16, jnp.int32
     dma = pltpu.SemaphoreType.DMA
     chunks = ni // CHUNK
-    residual = pl.pallas_call(
+    done = ni - CHUNK
+    vmem = pl.BlockSpec(memory_space=pltpu.VMEM)
+    smem = pl.BlockSpec(memory_space=pltpu.SMEM)
+    hbm = pl.BlockSpec(memory_space=pltpu.HBM)
+    held = pl.pallas_call(
         residual_kernel,
-        out_shape=pltpu.VMEM((ni, rows, width), f32),
-        in_specs=[pl.BlockSpec(memory_space=pltpu.HBM)] * 8
-        + [pl.BlockSpec(memory_space=pltpu.SMEM)],
-        out_specs=pl.BlockSpec(memory_space=pltpu.VMEM),
+        out_shape=(
+            pltpu.VMEM((done, rows, width), f32),
+            pltpu.VMEM((ni * rows, width), bf16),
+            pltpu.VMEM((rank, width), bf16),
+            pltpu.VMEM((ni, rank, rows), bf16),
+            pltpu.VMEM((1, width), f32),
+            pltpu.VMEM((rows, rows), f32),
+        ),
+        in_specs=[hbm] * 8 + [smem],
+        out_specs=(vmem,) * 6,
         scratch_shapes=[
             pltpu.VMEM((tiles_here, TILE, rank), bf16),
             pltpu.VMEM((1, tiles), i32),
             pltpu.VMEM(domains.shape, i32),
-            pltpu.VMEM((ni * rows, width), bf16),
             pltpu.VMEM((blk, rank), bf16),
             pltpu.VMEM((3, blk), bf16),
             pltpu.VMEM((lines, 2 * TILE), f32),
@@ -426,11 +449,9 @@
             pltpu.VMEM((8, 128), i32),
             pltpu.SMEM((8, 128), i32),
             pltpu.VMEM((3, blk, 128), f32),
-            pltpu.VMEM((1, width), f32),
-            pltpu.VMEM((rows, rows), f32),
             pltpu.VMEM((CAP // 2, rank, 2 * TILE), bf16),
-            pltpu.VMEM((PLANE * CAP // 2, blk, 2 * TILE), bf16),
-            pltpu.VMEM((rank, width), bf16),
+            pltpu.VMEM((PLANE * CAP // 2, blk // 2, 2 * TILE), bf16),
+            pltpu.VMEM((PLANE * CAP // 2, blk // 2, 2 * TILE), bf16),
             pltpu.VMEM((ni, rank, rows), bf16),
             pltpu.VMEM((ni, blk, width), bf16),
             pltpu.VMEM((ni, blk, rank), bf16),
@@ -438,10 +459,9 @@
             pltpu.VMEM((ni, blk, rank), bf16),
             pltpu.VMEM((CHUNK * blk, rank), bf16),
             pltpu.VMEM((ni, blk, width), bf16),
-            pltpu.VMEM((ni, rank, rows), bf16),
             dma((8,)),
             dma,
-            dma,
+            dma((2,)),
             dma((40,)),
             dma((40,)),
             dma,
@@ -453,7 +473,7 @@
             dma((chunks,)),
         ],
         compiler_params=pltpu.CompilerParams(
-            collective_id=0, has_side_effects=True, vmem_limit_bytes=48 * 2**20
+            collective_id=0, has_side_effects=True, vmem_limit_bytes=40 * 2**20
         ),
     )(
         factor.reshape(tiles_here, TILE, rank),
@@ -466,6 +486,18 @@
         occ_i,
         occ_j,
     )
+    residual = pl.pallas_call(
+        last_kernel,
+        out_shape=jax.ShapeDtypeStruct((ni, rows, width), f32),
+        in_specs=[smem] + [vmem] * 6,
+        out_specs=hbm,
+        scratch_shapes=[
+            pltpu.VMEM((CHUNK, rows, width), f32),
+            dma((done,)),
+            dma((len(ladder_steps(width)),)),
+        ],
+        compiler_params=pltpu.CompilerParams(vmem_limit_bytes=16 * 2**20),
+    )(occ_i, *held)
     return residual[None]
 
 

time: 95.1 us -> 91.4 us (0.961)
  local copies, waits for them, and re-layouts: 3.4 us -> 0.01 us
    unnamed x1 -> x2, local copies, waits for them, and re-layouts: 3.4 us -> 0.01 us
    pallas_call x1 -> x2, Pallas kernels: 91 us -> 90.6 us  [the longest x1 86.7 us: on_device(): pl.pallas_call(residual_kernel, out_shape=(pltpu.VMEM((done, rows, width)...]
where the time goes in v3:
time: 91.4 us; the launch traced here: 91.2 us
  Pallas kernels  90.6 us (99%)
    pallas_call x1, Pallas kernels, on_device(): pl.pallas_call(residual_kernel, out_shape=(pltpu.VMEM((done, rows, width)...  86.7 us
    pallas_call x1, Pallas kernels, on_device(): pl.pallas_call(last_kernel, out_shape=jax.ShapeDtypeStruct((ni, rows, wid...  3.91 us

profile of v3, /device:TPU:1, one launch (start us, length us, event | category | flops | bytes accessed | tf_op | source)
XLA Modules:
  0.0 91.2 jit_solution(3532787992778572055)
XLA Ops:
  0.0 0.0 copy-start
  0.7 86.7 %shard_map.91 = (f32[6,128,2048]{2,1,0:T(8,128)S(1)}, bf16[1024,2048]{1,0:T(8,128)(2,1)S(1)}, bf16[1024,2048]{1,0:T(8,128)(2,1)S(1)}, bf16[8,1024,128]{2,1,0:T(8...) custom-call(bf16[8,64,1024]{2,1,0:T(8,128)(2,1)} %bitcast.7, s32[1,128]{1,0:T(1,128)} %bitcast.10, ...), custom_call_target="tpu_custom_call" | custom-call | tf_op jit(solution)/shard_map/pallas_call | solution.py:429
  87.3 0.0 copy-done
  87.3 3.9 %shard_map.92 = f32[8,128,2048]{2,1,0:T(8,128)} custom-call(f32[8]{0:T(128)S(1)} %copy-done, f32[6,128,2048]{2,1,0:T(8,128)S(1)} %get-tuple-element.11.ladder, bf16[1024,2048]{1,0:T(8,128)(2,1)S(1)} %get-tuple-element.12.amp, bf16[1024,2048]{1,0:T(8,128)(2,1)S(1)} %get-tuple-element.13.dt, bf16[8,1024,128]{2,1,0:T(8,128)(2,1)S(1)} %get-tuple-element.14.recvb, ...), custom_call_target="tpu_custom_call" | custom-call | tf_op jit(solution)/shard_map/pallas_call | solution.py:489
Async XLA Ops:
  0.0 87.3 %copy-start = (f32[8]{0:T(128)S(1)}, f32[8]{0:T(128)}, u32[]{:S(2)}) copy-start(f32[8]{0:T(128)} %occ_i.1) | copy-start | bytes 100

commit v4 on v3

--- a/solution.py
+++ b/solution.py
@@ -10,6 +10,7 @@
 SIDE = 4
 PLANE = SIDE * SIDE
 CHUNK = 2
+SHARE = 16
 MESH = pl.DeviceIdType.MESH
 NT = (((1,), (1,)), ((), ()))
 NN = (((1,), (0,)), ((), ()))
@@ -82,6 +83,10 @@
     table,
     where,
     columns,
+    all_slots,
+    slot_lists,
+    full,
+    ready,
     pack,
     got_up,
     got_low,
@@ -93,6 +98,12 @@
     dressed,
     bbuf,
     io_sem,
+    slot_send,
+    slot_recv,
+    full_send,
+    full_recv,
+    share_out,
+    share_in,
     pack_sem,
     got_sem,
     ag_send,
@@ -127,8 +138,11 @@
             barrier, inc=1, device_id=(pair, lax.rem(me + s, PLANE)), device_id_type=MESH
         )
 
-    pl.semaphore_signal(barrier, inc=1, device_id=(after, me), device_id_type=MESH)
-    pl.semaphore_signal(barrier, inc=1, device_id=(before, me), device_id_type=MESH)
+    @pl.loop(1, pairs)
+    def _(s):
+        pl.semaphore_signal(
+            barrier, inc=1, device_id=(lax.rem(pair + s, pairs), me), device_id_type=MESH
+        )
 
     def fetch(k, src, dst):
         copy = pltpu.make_async_copy(src, dst, io_sem.at[k])
@@ -177,6 +191,8 @@
     table[4:5, :] = mine
     table[5:8, :] = jnp.zeros((3, 128), i32)
     scalars = fetch(0, table, where)
+    all_slots[pair] = jnp.zeros((1, 128), i32)
+    all_slots[pair, :, 0:in_domain] = slot_row
     scalars.wait()
 
     get_factor.wait()
@@ -184,13 +200,47 @@
         two = jnp.concatenate([factor[where[4, 2 * c]], factor[where[4, 2 * c + 1]]], axis=0)
         pack[c] = two.T
 
-    pl.semaphore_wait(barrier, PLANE + 1)
-
-    hb, qb = blk // 2, blk // 4
+    keep = blk - SHARE
+    per = PLANE // pairs
+    rank_cols = pl.ds(pl.multiple_of(pair * per * blk, per * blk), per * blk)
+    wide = factor[:, :, rank_cols].reshape(tiles_here * TILE, per * blk).T
+    wide = jnp.concatenate([wide[k * blk + keep : (k + 1) * blk] for k in range(per)], axis=0)
+    two_here = tiles_here // 2
+    for k in range(two_here):
+        full[me * two_here + k] = wide[:, k * 2 * TILE : (k + 1) * 2 * TILE]
+
+    pl.semaphore_wait(barrier, PLANE + pairs - 2)
+
+    hs = per * SHARE // 2
+
+    @pl.loop(1, pairs)
+    def _(s):
+        pltpu.make_async_remote_copy(
+            all_slots.at[pair], all_slots.at[pair], slot_send, slot_recv,
+            device_id=(lax.rem(pair + s, pairs), me), device_id_type=MESH,
+        ).start()
+
+    def share_send(first, n, h, sem, to):
+        part = full.at[pl.ds(first, n), h * hs : (h + 1) * hs, :]
+        pltpu.make_async_remote_copy(
+            part, part, full_send, full_recv.at[sem], device_id=(pair, to), device_id_type=MESH
+        ).start()
+
+    def to_x(s):
+        return y * SIDE + lax.rem(x + s, SIDE)
+
+    def to_y(s):
+        return lax.rem(y + s, SIDE) * SIDE + x
+
+    for s in range(1, SIDE):
+        share_send(me * two_here, two_here, 0, 0, to_x(s))
+        share_send(me * two_here, two_here, 1, 1, to_y(s))
+
     got = (got_up, got_low)
+    offs = (0, got_up.shape[1])
 
     def pack_part(d, h):
-        return pack.at[:, pl.ds(pl.multiple_of(d * blk + h * hb, hb), hb), :]
+        return pack.at[:, pl.ds(pl.multiple_of(d * blk + offs[h], 16), got[h].shape[1]), :]
 
     for h in range(2):
         here = got[h].at[pl.ds(me * (CAP // 2), CAP // 2)]
@@ -225,11 +275,23 @@
         line = weight[d : d + 1, :].astype(f32) * has[d]
         columns[d] = jnp.broadcast_to(line, (128, blk)).T
 
+    def share_landed(n, h, sem):
+        part = full.at[pl.ds(0, n), h * hs : (h + 1) * hs, :]
+        pltpu.make_async_copy(part, part, full_recv.at[sem]).wait()
+
+    share_landed((SIDE - 1) * two_here, 0, 0)
+    for s in range(1, SIDE):
+        share_send(y * SIDE * two_here, SIDE * two_here, 0, 2, to_y(s))
+    share_landed((SIDE - 1) * two_here, 1, 1)
+    for s in range(1, SIDE):
+        for k in range(SIDE):
+            share_send((k * SIDE + x) * two_here, two_here, 1, 3, to_x(s))
+
     own = pl.ds(pl.multiple_of(me * blk, blk), blk)
 
     def arrange(h):
         pltpu.make_async_copy(got[h], got[h], got_sem.at[h]).wait()
-        lines = pl.ds(pl.multiple_of(me * blk + h * hb, hb), hb)
+        lines = pl.ds(pl.multiple_of(me * blk + offs[h], 16), got[h].shape[1])
         for u in range(in_domain // 2):
             dt[lines, u * 2 * TILE : (u + 1) * 2 * TILE] = jnp.concatenate(
                 [halves(got[h][where[0, t]], where[1, t]) for t in (2 * u, 2 * u + 1)], axis=1
@@ -254,10 +316,10 @@
         else:
             block, to = at(h, s, -sign), at(h, 0, sign)
         if kind in ("a1", "b1"):
-            off, n = h * hb, hb
+            off, n = h * (width // 2), width // 2
         else:
-            off, n = h * hb + (0 if sign > 0 else qb), qb
-        part = dt.at[pl.ds(pl.multiple_of(block * blk + off, qb), n), :]
+            off, n = h * (width // 2) + (0 if sign > 0 else width // 4), width // 4
+        part = dt.at[pl.ds(pl.multiple_of(block * blk, blk), keep), off : off + n]
         return pltpu.make_async_remote_copy(
             part, part, ag_send.at[k], ag_recv.at[k], device_id=(pair, to), device_id_type=MESH
         )
@@ -305,11 +367,42 @@
                 d,
             )
 
-    for h in (0, 1):
-        arrange(h)
-        for kind in ("a1", "b1"):
-            for sign in (1, -1):
-                message(kind, h, 0, sign).start()
+    arrange(0)
+    arrange(1)
+    each("a1", (0,), go)
+    each("b1", (0,), go)
+
+    pltpu.make_async_copy(
+        all_slots.at[pl.ds(0, pairs - 1)], all_slots.at[pl.ds(0, pairs - 1)], slot_recv
+    ).wait()
+    lists = fetch(0, all_slots, slot_lists)
+    share_landed((SIDE - 1) * SIDE * two_here, 0, 2)
+    share_landed((SIDE - 1) * SIDE * two_here, 1, 3)
+    lists.wait()
+
+    @pl.loop(0, pairs)
+    def _(k):
+        p = lax.rem(pair + pairs // 2 + k, pairs)
+        for u in range(in_domain // 2):
+            both = [slot_lists[p, 0, t] for t in (2 * u, 2 * u + 1)]
+            ready[p, :, u * 2 * TILE : (u + 1) * 2 * TILE] = jnp.concatenate(
+                [halves(full[lax.div(s, 2)], lax.rem(s, 2)) for s in both], axis=1
+            )
+        for b in range(per):
+            src = ready.at[p, b * SHARE : (b + 1) * SHARE, :]
+            start = pl.multiple_of((pair * per + b) * blk + keep, SHARE)
+            dst = dt.at[pl.ds(start, SHARE), :]
+
+            @pl.when(p != pair)
+            def _():
+                pltpu.make_async_remote_copy(
+                    src, dst, share_out, share_in, device_id=(p, me), device_id_type=MESH
+                ).start()
+
+            @pl.when(p == pair)
+            def _():
+                pltpu.make_async_copy(src, dst, share_in).start()
+
     for h in (0, 1):
         for sign in (1, -1):
             message("a1", h, 0, sign).wait_recv()
@@ -326,6 +419,8 @@
     each("b2", (2,), go)
 
     each("b2", (1, -1, 2), landed)
+    all_shares = dt.at[pl.ds(0, PLANE * SHARE), :]
+    pltpu.make_async_copy(all_shares, all_shares, share_in).wait()
     get_amp.wait()
 
     @pl.loop(0, chunks)
@@ -402,7 +497,11 @@
     def sent(ref, sem):
         pltpu.make_async_copy(ref, ref, sem).wait()
 
-    sent(pack.at[:, pl.ds(blk, (PLANE - 1) * blk), :], pack_sem)
+    sent(pack.at[:, pl.ds(0, (PLANE - 1) * keep), :], pack_sem)
+    sent(all_slots.at[pl.ds(0, pairs - 1)], slot_send)
+    units = (SIDE - 1) * (2 + 2 * SIDE) * two_here
+    sent(full.at[pl.ds(0, units // 2)], full_send)
+    sent(ready.at[pl.ds(0, pairs - 1)], share_out)
     sent(hbuf.at[:, pl.ds(blk, (PLANE - 1) * blk), :], h_send)
     sent(proj, p_send.at[0])
     sent(proj, p_send.at[1])
@@ -412,6 +511,7 @@
 
 
 def on_device(amplitudes, factor, home, domains, coupling, hole_weight, virt_energy, occ_i, occ_j):
+    pairs = lax.axis_size("pair")
     ni, rows, width = amplitudes.shape[1:]
     stored, rank = factor.shape
     tiles_here = stored // TILE
@@ -449,9 +549,13 @@
             pltpu.VMEM((8, 128), i32),
             pltpu.SMEM((8, 128), i32),
             pltpu.VMEM((3, blk, 128), f32),
+            pltpu.VMEM((pairs, 1, 128), i32),
+            pltpu.SMEM((pairs, 1, 128), i32),
+            pltpu.VMEM((tiles // 2, PLANE * SHARE // pairs, 2 * TILE), bf16),
+            pltpu.VMEM((pairs, PLANE * SHARE // pairs, width), bf16),
             pltpu.VMEM((CAP // 2, rank, 2 * TILE), bf16),
-            pltpu.VMEM((PLANE * CAP // 2, blk // 2, 2 * TILE), bf16),
-            pltpu.VMEM((PLANE * CAP // 2, blk // 2, 2 * TILE), bf16),
+            pltpu.VMEM((PLANE * CAP // 2, 32, 2 * TILE), bf16),
+            pltpu.VMEM((PLANE * CAP // 2, blk - SHARE - 32, 2 * TILE), bf16),
             pltpu.VMEM((ni, rank, rows), bf16),
             pltpu.VMEM((ni, blk, width), bf16),
             pltpu.VMEM((ni, blk, rank), bf16),
@@ -460,6 +564,12 @@
             pltpu.VMEM((CHUNK * blk, rank), bf16),
             pltpu.VMEM((ni, blk, width), bf16),
             dma((8,)),
+            dma,
+            dma,
+            dma,
+            dma((4,)),
+            dma,
+            dma,
             dma,
             dma((2,)),
             dma((40,)),

time: 91.4 us -> 88.9 us (0.973); the launches traced: 91.2 us -> 87.7 us
  Pallas kernels: 90.6 us -> 87 us
    pallas_call x1, Pallas kernels: 86.7 us -> 83.1 us  [on_device(): pl.pallas_call(residual_kernel, out_shape=(pltpu.VMEM((done, rows, width)...]
where the time goes in v4:
time: 88.9 us; the launch traced here: 87.7 us
  Pallas kernels  87 us (98%)
    pallas_call x1, Pallas kernels, on_device(): pl.pallas_call(residual_kernel, out_shape=(pltpu.VMEM((done, rows, width)...  83.1 us
    pallas_call x1, Pallas kernels, on_device(): pl.pallas_call(last_kernel, out_shape=jax.ShapeDtypeStruct((ni, rows, wid...  3.91 us

profile of v4, /device:TPU:1, one launch (start us, length us, event | category | flops | bytes accessed | tf_op | source)
XLA Modules:
  0.0 87.7 jit_solution(15835270256709099070)
XLA Ops:
  0.0 0.0 copy-start
  0.7 83.1 %shard_map.91 = (f32[6,128,2048]{2,1,0:T(8,128)S(1)}, bf16[1024,2048]{1,0:T(8,128)(2,1)S(1)}, bf16[1024,2048]{1,0:T(8,128)(2,1)S(1)}, bf16[8,1024,128]{2,1,0:T(8...) custom-call(bf16[8,64,1024]{2,1,0:T(8,128)(2,1)} %bitcast.7, s32[1,128]{1,0:T(1,128)} %bitcast.10, ...), custom_call_target="tpu_custom_call" | custom-call | tf_op jit(solution)/shard_map/pallas_call | solution.py:529
  83.8 0.0 copy-done
  83.8 3.9 %shard_map.92 = f32[8,128,2048]{2,1,0:T(8,128)} custom-call(f32[8]{0:T(128)S(1)} %copy-done, f32[6,128,2048]{2,1,0:T(8,128)S(1)} %get-tuple-element.11.ladder, bf16[1024,2048]{1,0:T(8,128)(2,1)S(1)} %get-tuple-element.12.amp, bf16[1024,2048]{1,0:T(8,128)(2,1)S(1)} %get-tuple-element.13.dt, bf16[8,1024,128]{2,1,0:T(8,128)(2,1)S(1)} %get-tuple-element.14.recvb, ...), custom_call_target="tpu_custom_call" | custom-call | tf_op jit(solution)/shard_map/pallas_call | solution.py:599
Async XLA Ops:
  0.0 83.8 %copy-start = (f32[8]{0:T(128)S(1)}, f32[8]{0:T(128)}, u32[]{:S(2)}) copy-start(f32[8]{0:T(128)} %occ_i.1) | copy-start | bytes 100

commit v5 on v4

--- a/solution.py
+++ b/solution.py
@@ -192,7 +192,8 @@
     table[5:8, :] = jnp.zeros((3, 128), i32)
     scalars = fetch(0, table, where)
     all_slots[pair] = jnp.zeros((1, 128), i32)
-    all_slots[pair, :, 0:in_domain] = slot_row
+    turn = lax.rem(slot_row + lax.broadcasted_iota(i32, (1, in_domain), 1), 2)
+    all_slots[pair, :, 0:in_domain] = lax.div(slot_row, 2) + turn * (tiles // 2)
     scalars.wait()
 
     get_factor.wait()
@@ -255,11 +256,28 @@
 
         pltpu.make_async_copy(pack_part(me, h), here, got_sem.at[h]).start()
 
+    def share_landed(n, h, sem):
+        part = full.at[pl.ds(0, n), h * hs : (h + 1) * hs, :]
+        pltpu.make_async_copy(part, part, full_recv.at[sem]).wait()
+
+    share_landed((SIDE - 1) * two_here, 0, 0)
+    for s in range(1, SIDE):
+        share_send(y * SIDE * two_here, SIDE * two_here, 0, 2, to_y(s))
+    share_landed((SIDE - 1) * two_here, 1, 1)
+    for s in range(1, SIDE):
+        for k in range(SIDE):
+            share_send((k * SIDE + x) * two_here, two_here, 1, 3, to_x(s))
+
     for copy in get_small:
         copy.wait()
 
     def halves(wide, second):
         return jnp.where(second == 1, wide[:, TILE:], wide[:, :TILE])
+
+    low = lax.broadcasted_iota(i32, (32, 2 * TILE), 1) < TILE
+
+    def swapped(wide):
+        return jnp.concatenate([wide[:, TILE:], wide[:, :TILE]], axis=1)
 
     def energy_of(t):
         return halves(energy[pl.ds(where[2, t], 1), :], where[3, t])
@@ -275,26 +293,19 @@
         line = weight[d : d + 1, :].astype(f32) * has[d]
         columns[d] = jnp.broadcast_to(line, (128, blk)).T
 
-    def share_landed(n, h, sem):
-        part = full.at[pl.ds(0, n), h * hs : (h + 1) * hs, :]
-        pltpu.make_async_copy(part, part, full_recv.at[sem]).wait()
-
-    share_landed((SIDE - 1) * two_here, 0, 0)
-    for s in range(1, SIDE):
-        share_send(y * SIDE * two_here, SIDE * two_here, 0, 2, to_y(s))
-    share_landed((SIDE - 1) * two_here, 1, 1)
-    for s in range(1, SIDE):
-        for k in range(SIDE):
-            share_send((k * SIDE + x) * two_here, two_here, 1, 3, to_x(s))
-
     own = pl.ds(pl.multiple_of(me * blk, blk), blk)
 
     def arrange(h):
         pltpu.make_async_copy(got[h], got[h], got_sem.at[h]).wait()
         lines = pl.ds(pl.multiple_of(me * blk + offs[h], 16), got[h].shape[1])
         for u in range(in_domain // 2):
-            dt[lines, u * 2 * TILE : (u + 1) * 2 * TILE] = jnp.concatenate(
-                [halves(got[h][where[0, t]], where[1, t]) for t in (2 * u, 2 * u + 1)], axis=1
+            even, odd = [
+                jnp.where(where[1, t] == t % 2, wide, swapped(wide))
+                for t in (2 * u, 2 * u + 1)
+                for wide in (got[h][where[0, t]],)
+            ]
+            dt[lines, u * 2 * TILE : (u + 1) * 2 * TILE] = jnp.where(
+                low[: even.shape[0]], even, odd
             )
 
     def device(dy, dx):
@@ -378,40 +389,47 @@
     lists = fetch(0, all_slots, slot_lists)
     share_landed((SIDE - 1) * SIDE * two_here, 0, 2)
     share_landed((SIDE - 1) * SIDE * two_here, 1, 3)
+    for k in range(tiles // 2):
+        full[tiles // 2 + k] = swapped(full[k])
     lists.wait()
 
-    @pl.loop(0, pairs)
-    def _(k):
-        p = lax.rem(pair + pairs // 2 + k, pairs)
-        for u in range(in_domain // 2):
-            both = [slot_lists[p, 0, t] for t in (2 * u, 2 * u + 1)]
-            ready[p, :, u * 2 * TILE : (u + 1) * 2 * TILE] = jnp.concatenate(
-                [halves(full[lax.div(s, 2)], lax.rem(s, 2)) for s in both], axis=1
-            )
-        for b in range(per):
-            src = ready.at[p, b * SHARE : (b + 1) * SHARE, :]
-            start = pl.multiple_of((pair * per + b) * blk + keep, SHARE)
-            dst = dt.at[pl.ds(start, SHARE), :]
-
-            @pl.when(p != pair)
-            def _():
-                pltpu.make_async_remote_copy(
-                    src, dst, share_out, share_in, device_id=(p, me), device_id_type=MESH
-                ).start()
-
-            @pl.when(p == pair)
-            def _():
-                pltpu.make_async_copy(src, dst, share_in).start()
-
+    def hand_out(first, last):
+        @pl.loop(first, last)
+        def _(k):
+            p = lax.rem(pair + pairs // 2 + k, pairs)
+
+            for u in range(in_domain // 2):
+                ready[p, :, u * 2 * TILE : (u + 1) * 2 * TILE] = jnp.where(
+                    low, full[slot_lists[p, 0, 2 * u]], full[slot_lists[p, 0, 2 * u + 1]]
+                )
+
+            for b in range(per):
+                src = ready.at[p, b * SHARE : (b + 1) * SHARE, :]
+                start = pl.multiple_of((pair * per + b) * blk + keep, SHARE)
+                dst = dt.at[pl.ds(start, SHARE), :]
+
+                @pl.when(p != pair)
+                def _():
+                    pltpu.make_async_remote_copy(
+                        src, dst, share_out, share_in, device_id=(p, me), device_id_type=MESH
+                    ).start()
+
+                @pl.when(p == pair)
+                def _():
+                    pltpu.make_async_copy(src, dst, share_in).start()
+
+    hand_out(0, 3)
     for h in (0, 1):
         for sign in (1, -1):
             message("a1", h, 0, sign).wait_recv()
             message("a2", h, 0, sign).start()
     each("b1", (1, -1), go)
+    hand_out(3, 5)
     each("b1", (0,), landed)
     each("b2", (0,), go)
     each("a2", (0,), landed)
     each("b1", (2,), go)
+    hand_out(5, pairs)
     each("b2", (0,), landed)
     each("b1", (1, -1), landed)
     each("b2", (1, -1), go)
@@ -551,7 +569,7 @@
             pltpu.VMEM((3, blk, 128), f32),
             pltpu.VMEM((pairs, 1, 128), i32),
             pltpu.SMEM((pairs, 1, 128), i32),
-            pltpu.VMEM((tiles // 2, PLANE * SHARE // pairs, 2 * TILE), bf16),
+            pltpu.VMEM((tiles, PLANE * SHARE // pairs, 2 * TILE), bf16),
             pltpu.VMEM((pairs, PLANE * SHARE // pairs, width), bf16),
             pltpu.VMEM((CAP // 2, rank, 2 * TILE), bf16),
             pltpu.VMEM((PLANE * CAP // 2, 32, 2 * TILE), bf16),

time: 88.9 us -> 88.2 us (level); the launches traced: 87.7 us -> 88.1 us
  no operation moved by 1% of the time
where the time goes in v5:
time: 88.2 us; the launch traced here: 88.1 us
  Pallas kernels  87.4 us (99%)
    pallas_call x1, Pallas kernels, on_device(): pl.pallas_call(residual_kernel, out_shape=(pltpu.VMEM((done, rows, width)...  83.5 us
    pallas_call x1, Pallas kernels, on_device(): pl.pallas_call(last_kernel, out_shape=jax.ShapeDtypeStruct((ni, rows, wid...  3.91 us

profile of v5, /device:TPU:1, one launch (start us, length us, event | category | flops | bytes accessed | tf_op | source)
XLA Modules:
  0.0 88.1 jit_solution(10289532826901559516)
XLA Ops:
  0.0 0.0 copy-start
  0.7 83.5 %shard_map.91 = (f32[6,128,2048]{2,1,0:T(8,128)S(1)}, bf16[1024,2048]{1,0:T(8,128)(2,1)S(1)}, bf16[1024,2048]{1,0:T(8,128)(2,1)S(1)}, bf16[8,1024,128]{2,1,0:T(8...) custom-call(bf16[8,64,1024]{2,1,0:T(8,128)(2,1)} %bitcast.7, s32[1,128]{1,0:T(1,128)} %bitcast.10, ...), custom_call_target="tpu_custom_call" | custom-call | tf_op jit(solution)/shard_map/pallas_call | solution.py:547
  84.2 0.0 copy-done
  84.2 3.9 %shard_map.92 = f32[8,128,2048]{2,1,0:T(8,128)} custom-call(f32[8]{0:T(128)S(1)} %copy-done, f32[6,128,2048]{2,1,0:T(8,128)S(1)} %get-tuple-element.11.ladder, bf16[1024,2048]{1,0:T(8,128)(2,1)S(1)} %get-tuple-element.12.amp, bf16[1024,2048]{1,0:T(8,128)(2,1)S(1)} %get-tuple-element.13.dt, bf16[8,1024,128]{2,1,0:T(8,128)(2,1)S(1)} %get-tuple-element.14.recvb, ...), custom_call_target="tpu_custom_call" | custom-call | tf_op jit(solution)/shard_map/pallas_call | solution.py:617
Async XLA Ops:
  0.0 84.2 %copy-start = (f32[8]{0:T(128)S(1)}, f32[8]{0:T(128)}, u32[]{:S(2)}) copy-start(f32[8]{0:T(128)} %occ_i.1) | copy-start | bytes 100

commit v6 on v5

--- a/solution.py
+++ b/solution.py
@@ -89,7 +89,6 @@
     ready,
     pack,
     got_up,
-    got_low,
     hbuf,
     recvh,
     proj,
@@ -237,13 +236,13 @@
         share_send(me * two_here, two_here, 0, 0, to_x(s))
         share_send(me * two_here, two_here, 1, 1, to_y(s))
 
-    got = (got_up, got_low)
-    offs = (0, got_up.shape[1])
+    got = (got_up,)
+    offs = (0,)
 
     def pack_part(d, h):
         return pack.at[:, pl.ds(pl.multiple_of(d * blk + offs[h], 16), got[h].shape[1]), :]
 
-    for h in range(2):
+    for h in range(1):
         here = got[h].at[pl.ds(me * (CAP // 2), CAP // 2)]
 
         @pl.loop(1, PLANE)
@@ -274,7 +273,7 @@
     def halves(wide, second):
         return jnp.where(second == 1, wide[:, TILE:], wide[:, :TILE])
 
-    low = lax.broadcasted_iota(i32, (32, 2 * TILE), 1) < TILE
+    low = lax.broadcasted_iota(i32, (blk, 2 * TILE), 1) < TILE
 
     def swapped(wide):
         return jnp.concatenate([wide[:, TILE:], wide[:, :TILE]], axis=1)
@@ -379,7 +378,6 @@
             )
 
     arrange(0)
-    arrange(1)
     each("a1", (0,), go)
     each("b1", (0,), go)
 
@@ -400,7 +398,9 @@
 
             for u in range(in_domain // 2):
                 ready[p, :, u * 2 * TILE : (u + 1) * 2 * TILE] = jnp.where(
-                    low, full[slot_lists[p, 0, 2 * u]], full[slot_lists[p, 0, 2 * u + 1]]
+                    low[: full.shape[1]],
+                    full[slot_lists[p, 0, 2 * u]],
+                    full[slot_lists[p, 0, 2 * u + 1]],
                 )
 
             for b in range(per):
@@ -445,7 +445,7 @@
     def _(c):
         @pl.loop(0, SIDE)
         def _(k):
-            half(c, lax.rem(y + k, SIDE))
+            half(c, lax.rem(y + k + 1, SIDE))
 
     def project(c):
         now = pl.ds(c * CHUNK, CHUNK)
@@ -482,7 +482,7 @@
 
         @pl.loop(0, SIDE)
         def _(k):
-            r = lax.rem(y + k, SIDE)
+            r = lax.rem(y + k + 1, SIDE)
             cols = pl.ds(pl.multiple_of(r * SIDE * rows, SIDE * rows), SIDE * rows)
             part = dot(dressed[...], dt[:, cols], NN).astype(bf16)
             bbuf[now, :, cols] = part.reshape(CHUNK, blk, SIDE * rows)
@@ -572,8 +572,7 @@
             pltpu.VMEM((tiles, PLANE * SHARE // pairs, 2 * TILE), bf16),
             pltpu.VMEM((pairs, PLANE * SHARE // pairs, width), bf16),
             pltpu.VMEM((CAP // 2, rank, 2 * TILE), bf16),
-            pltpu.VMEM((PLANE * CAP // 2, 32, 2 * TILE), bf16),
-            pltpu.VMEM((PLANE * CAP // 2, blk - SHARE - 32, 2 * TILE), bf16),
+            pltpu.VMEM((PLANE * CAP // 2, blk - SHARE, 2 * TILE), bf16),
             pltpu.VMEM((ni, rank, rows), bf16),
             pltpu.VMEM((ni, blk, width), bf16),
             pltpu.VMEM((ni, blk, rank), bf16),

time: 88.2 us -> 87.4 us (level)
  no operation moved by 1% of the time
where the time goes in v6:
time: 87.4 us; the launch traced here: 87.2 us
  Pallas kernels  86.6 us (99%)
    pallas_call x1, Pallas kernels, on_device(): pl.pallas_call(residual_kernel, out_shape=(pltpu.VMEM((done, rows, width)...  82.6 us
    pallas_call x1, Pallas kernels, on_device(): pl.pallas_call(last_kernel, out_shape=jax.ShapeDtypeStruct((ni, rows, wid...  3.91 us

profile of v6, /device:TPU:1, one launch (start us, length us, event | category | flops | bytes accessed | tf_op | source)
XLA Modules:
  0.0 87.2 jit_solution(9578766760525382085)
XLA Ops:
  0.0 0.0 copy-start
  0.7 82.6 %shard_map.91 = (f32[6,128,2048]{2,1,0:T(8,128)S(1)}, bf16[1024,2048]{1,0:T(8,128)(2,1)S(1)}, bf16[1024,2048]{1,0:T(8,128)(2,1)S(1)}, bf16[8,1024,128]{2,1,0:T(8...) custom-call(bf16[8,64,1024]{2,1,0:T(8,128)(2,1)} %bitcast.7, s32[1,128]{1,0:T(1,128)} %bitcast.10, ...), custom_call_target="tpu_custom_call" | custom-call | tf_op jit(solution)/shard_map/pallas_call | solution.py:547
  83.3 0.0 copy-done
  83.3 3.9 %shard_map.92 = f32[8,128,2048]{2,1,0:T(8,128)} custom-call(f32[8]{0:T(128)S(1)} %copy-done, f32[6,128,2048]{2,1,0:T(8,128)S(1)} %get-tuple-element.11.ladder, bf16[1024,2048]{1,0:T(8,128)(2,1)S(1)} %get-tuple-element.12.amp, bf16[1024,2048]{1,0:T(8,128)(2,1)S(1)} %get-tuple-element.13.dt, bf16[8,1024,128]{2,1,0:T(8,128)(2,1)S(1)} %get-tuple-element.14.recvb, ...), custom_call_target="tpu_custom_call" | custom-call | tf_op jit(solution)/shard_map/pallas_call | solution.py:616
Async XLA Ops:
  0.0 83.3 %copy-start = (f32[8]{0:T(128)S(1)}, f32[8]{0:T(128)}, u32[]{:S(2)}) copy-start(f32[8]{0:T(128)} %occ_i.1) | copy-start | bytes 100

commit v7 on v6

--- a/solution.py
+++ b/solution.py
@@ -267,30 +267,10 @@
         for k in range(SIDE):
             share_send((k * SIDE + x) * two_here, two_here, 1, 3, to_x(s))
 
-    for copy in get_small:
-        copy.wait()
-
-    def halves(wide, second):
-        return jnp.where(second == 1, wide[:, TILE:], wide[:, :TILE])
-
     low = lax.broadcasted_iota(i32, (blk, 2 * TILE), 1) < TILE
 
     def swapped(wide):
         return jnp.concatenate([wide[:, TILE:], wide[:, :TILE]], axis=1)
-
-    def energy_of(t):
-        return halves(energy[pl.ds(where[2, t], 1), :], where[3, t])
-
-    for u in range(in_domain // 2):
-        col[:, u * 2 * TILE : (u + 1) * 2 * TILE] = jnp.concatenate(
-            [energy_of(2 * u), energy_of(2 * u + 1)], axis=1
-        )
-    here_energy = col[:, pl.ds(pl.multiple_of(me * rows, rows), rows)]
-    row[...] = jnp.broadcast_to(here_energy, (rows, rows)).T - occ_j[0]
-    has = (jnp.where(pair > 0, 1.0, 0.0), 1.0, jnp.where(pair < pairs - 1, 1.0, 0.0))
-    for d in range(3):
-        line = weight[d : d + 1, :].astype(f32) * has[d]
-        columns[d] = jnp.broadcast_to(line, (128, blk)).T
 
     own = pl.ds(pl.multiple_of(me * blk, blk), blk)
 
@@ -430,6 +410,27 @@
     each("a2", (0,), landed)
     each("b1", (2,), go)
     hand_out(5, pairs)
+
+    for copy in get_small:
+        copy.wait()
+
+    def halves(wide, second):
+        return jnp.where(second == 1, wide[:, TILE:], wide[:, :TILE])
+
+    def energy_of(t):
+        return halves(energy[pl.ds(where[2, t], 1), :], where[3, t])
+
+    for u in range(in_domain // 2):
+        col[:, u * 2 * TILE : (u + 1) * 2 * TILE] = jnp.concatenate(
+            [energy_of(2 * u), energy_of(2 * u + 1)], axis=1
+        )
+    here_energy = col[:, pl.ds(pl.multiple_of(me * rows, rows), rows)]
+    row[...] = jnp.broadcast_to(here_energy, (rows, rows)).T - occ_j[0]
+    has = (jnp.where(pair > 0, 1.0, 0.0), 1.0, jnp.where(pair < pairs - 1, 1.0, 0.0))
+    for d in range(3):
+        line = weight[d : d + 1, :].astype(f32) * has[d]
+        columns[d] = jnp.broadcast_to(line, (128, blk)).T
+
     each("b2", (0,), landed)
     each("b1", (1, -1), landed)
     each("b2", (1, -1), go)

time: 87.4 us -> 87.4 us (level)
  no operation moved by 1% of the time
where the time goes in v7:
time: 87.4 us; the launch traced here: 87.3 us
  Pallas kernels  86.6 us (99%)
    pallas_call x1, Pallas kernels, on_device(): pl.pallas_call(residual_kernel, out_shape=(pltpu.VMEM((done, rows, width)...  82.7 us
    pallas_call x1, Pallas kernels, on_device(): pl.pallas_call(last_kernel, out_shape=jax.ShapeDtypeStruct((ni, rows, wid...  3.91 us

profile of v7, /device:TPU:1, one launch (start us, length us, event | category | flops | bytes accessed | tf_op | source)
XLA Modules:
  0.0 87.3 jit_solution(10362378004791977869)
XLA Ops:
  0.0 0.0 copy-start
  0.7 82.7 %shard_map.91 = (f32[6,128,2048]{2,1,0:T(8,128)S(1)}, bf16[1024,2048]{1,0:T(8,128)(2,1)S(1)}, bf16[1024,2048]{1,0:T(8,128)(2,1)S(1)}, bf16[8,1024,128]{2,1,0:T(8...) custom-call(bf16[8,64,1024]{2,1,0:T(8,128)(2,1)} %bitcast.7, s32[1,128]{1,0:T(1,128)} %bitcast.10, ...), custom_call_target="tpu_custom_call" | custom-call | tf_op jit(solution)/shard_map/pallas_call | solution.py:548
  83.4 0.0 copy-done
  83.4 3.9 %shard_map.92 = f32[8,128,2048]{2,1,0:T(8,128)} custom-call(f32[8]{0:T(128)S(1)} %copy-done, f32[6,128,2048]{2,1,0:T(8,128)S(1)} %get-tuple-element.11.ladder, bf16[1024,2048]{1,0:T(8,128)(2,1)S(1)} %get-tuple-element.12.amp, bf16[1024,2048]{1,0:T(8,128)(2,1)S(1)} %get-tuple-element.13.dt, bf16[8,1024,128]{2,1,0:T(8,128)(2,1)S(1)} %get-tuple-element.14.recvb, ...), custom_call_target="tpu_custom_call" | custom-call | tf_op jit(solution)/shard_map/pallas_call | solution.py:617
Async XLA Ops:
  0.0 83.4 %copy-start = (f32[8]{0:T(128)S(1)}, f32[8]{0:T(128)}, u32[]{:S(2)}) copy-start(f32[8]{0:T(128)} %occ_i.1) | copy-start | bytes 100

commit v8 on v6

--- a/solution.py
+++ b/solution.py
@@ -42,7 +42,7 @@
 def last_kernel(occ_i, ladder, amp, dt, recvb, col, row, out_hbm, last, sem, last_sem):
     done = ladder.shape[0]
     c = done // CHUNK
-    copies = [pltpu.make_async_copy(ladder.at[i], out_hbm.at[i], sem.at[i]) for i in range(done)]
+    copies = [pltpu.make_async_copy(ladder, out_hbm.at[pl.ds(0, done)], sem.at[0])]
     for copy in copies:
         copy.start()
     left = ladder_left(recvb, c)

time: 87.4 us -> 87.5 us (level)
  no operation moved by 1% of the time
where the time goes in v8:
time: 87.5 us; the launch traced here: 87.3 us
  Pallas kernels  86.6 us (99%)
    pallas_call x1, Pallas kernels, on_device(): pl.pallas_call(residual_kernel, out_shape=(pltpu.VMEM((done, rows, width)...  82.7 us
    pallas_call x1, Pallas kernels, on_device(): pl.pallas_call(last_kernel, out_shape=jax.ShapeDtypeStruct((ni, rows, wid...  3.97 us

profile of v8, /device:TPU:1, one launch (start us, length us, event | category | flops | bytes accessed | tf_op | source)
XLA Modules:
  0.0 87.3 jit_solution(2994293671711081704)
XLA Ops:
  0.0 0.0 copy-start
  0.7 82.7 %shard_map.91 = (f32[6,128,2048]{2,1,0:T(8,128)S(1)}, bf16[1024,2048]{1,0:T(8,128)(2,1)S(1)}, bf16[1024,2048]{1,0:T(8,128)(2,1)S(1)}, bf16[8,1024,128]{2,1,0:T(8...) custom-call(bf16[8,64,1024]{2,1,0:T(8,128)(2,1)} %bitcast.7, s32[1,128]{1,0:T(1,128)} %bitcast.10, ...), custom_call_target="tpu_custom_call" | custom-call | tf_op jit(solution)/shard_map/pallas_call | solution.py:547
  83.3 0.0 copy-done
  83.4 4.0 %shard_map.92 = f32[8,128,2048]{2,1,0:T(8,128)} custom-call(f32[8]{0:T(128)S(1)} %copy-done, f32[6,128,2048]{2,1,0:T(8,128)S(1)} %get-tuple-element.11.ladder, bf16[1024,2048]{1,0:T(8,128)(2,1)S(1)} %get-tuple-element.12.amp, bf16[1024,2048]{1,0:T(8,128)(2,1)S(1)} %get-tuple-element.13.dt, bf16[8,1024,128]{2,1,0:T(8,128)(2,1)S(1)} %get-tuple-element.14.recvb, ...), custom_call_target="tpu_custom_call" | custom-call | tf_op jit(solution)/shard_map/pallas_call | solution.py:616
Async XLA Ops:
  0.0 83.3 %copy-start = (f32[8]{0:T(128)S(1)}, f32[8]{0:T(128)}, u32[]{:S(2)}) copy-start(f32[8]{0:T(128)} %occ_i.1) | copy-start | bytes 100
